TPU v7x, 128 devices: a whole 4x4x4 slice. The times are simulated.
128 devices in a mesh: seq: 16 (over x, y), head: 8 (over z, core).
Axes of the slice: x: 4, y: 4, z: 4, core: 2. Of those that a mesh axis runs over, the one named last changes fastest.
Arguments:
- query_proj: bfloat16 [49152, 5120], P('seq', 'head'), may hold values from -10 to 10
- key_proj: bfloat16 [49152, 5120], P('seq', 'head'), may hold values from -10 to 10
- value_proj: bfloat16 [49152, 5120], P('seq', 'head'), may hold values from -6 to 6
- query_gain: float32 [5120], P('head'), may hold values from 0.5 to 1.5
- key_gain: float32 [5120], P('head'), may hold values from 0.5 to 1.5
- head_class: int32 [40], P('head'), may hold values from 0 to 1, as said below
- spatial_mask: int32 [40, 12, 12], P('head'), may hold values 0 or 1
- temporal_mask: int32 [40, 8, 8], P('head'), may hold values 0 or 1
- location_order: int32 [1536], replicated, may hold values from 0 to 1535, each once
Outputs:
- attended: bfloat16 [49152, 5120], P('seq', 'head')
Inputs may be any that keep to these rules, and one draw needn't show every extreme that they name: `head_class`: in every aligned group of 5 consecutive heads exactly 4 are temporal (1), the others spatial (0).
All inputs are finite; a program needn't handle non-finite values. No bound on the sum of `spatial_mask` or of `temporal_mask` on one device may be relied on, other than what follows from the above.
Results may differ from a plain program's by a relative error of at most 0.001.
The roundings to bfloat16 on the way count: a program that leaves them out, or rounds other values in their place, can miss the bound.
Values may be sent and summed in bfloat16 or wider, within the bound.
No kernel may reach another device: no remote copies, remote signals or barrier semaphores. Data moves between devices by JAX's collectives and lax.ppermute only.
A program may use at most 128 MiB of HBM per device.

v0:
```python
import jax
import jax.numpy as jnp
from jax import lax
from jax.sharding import PartitionSpec as P

HEADS = 40
HEAD_DIM = 128
LOCATIONS = 1536
BLOCK = 128
WINDOW_SPAN = 32
GROUP = 5
TEMPORAL = 4


EPSILON = 1e-06


def expand_mask(block_mask):
    blocks = block_mask.shape[-1]
    diagonal = (
        jnp.arange(blocks, dtype=jnp.int32)[:, None] == jnp.arange(blocks, dtype=jnp.int32)[None, :]
    )
    kept_mask = (block_mask != 0) | diagonal
    widened = jnp.broadcast_to(kept_mask[:, None, :, None], (blocks, BLOCK, blocks, BLOCK))
    return widened.reshape(blocks * BLOCK, blocks * BLOCK)


def attend(queries, key_rows, values, allowed):
    scaling = queries.shape[-1] ** (-0.5)
    scores = (
        jnp.einsum("gqd,gkd->gqk", queries, key_rows, preferred_element_type=jnp.float32) * scaling
    )
    scores = jnp.where(allowed, scores, -jnp.inf)
    row_top = jnp.max(scores, axis=-1, keepdims=True)
    weights = jnp.where(allowed, jnp.exp(scores - row_top), 0.0)
    totals = jnp.sum(weights, axis=-1, keepdims=True)
    mixture = jnp.einsum(
        "gqk,gkd->gqd", weights.astype(jnp.bfloat16), values, preferred_element_type=jnp.float32
    )
    return (mixture / totals).astype(jnp.bfloat16)


def normalize(projected, gain_local, square_sums):
    factor = lax.rsqrt(square_sums / (HEADS * HEAD_DIM) + EPSILON)
    scaled = projected.astype(jnp.float32) * factor[:, None]
    return (scaled * gain_local).astype(jnp.bfloat16)


def per_head(query_heads, key_heads, value_heads, block_masks):

    def one_head(member):
        queries, key_rows, values, block_mask = member
        return attend(queries, key_rows, values, expand_mask(block_mask))

    return lax.map(one_head, (query_heads, key_heads, value_heads, block_masks))


def temporal_heads(relaid, block_masks):
    head_count, row_count, frame_count, feature_count = relaid[0].shape
    window_shape = (head_count, row_count // WINDOW_SPAN, WINDOW_SPAN * frame_count, feature_count)
    result = per_head(
        relaid[0].reshape(window_shape),
        relaid[1].reshape(window_shape),
        relaid[2].reshape(window_shape),
        block_masks,
    )
    return result.reshape(head_count, row_count, frame_count, feature_count)


def send_out(query_heads, key_heads, value_heads, temporal_index, location_order):

    def location_major(tensor):
        picked = jnp.take(tensor, temporal_index, axis=0)
        turned = jnp.swapaxes(picked, 1, 2)
        return jnp.take(turned, location_order, axis=1)

    moved = (location_major(query_heads), location_major(key_heads), location_major(value_heads))
    return (
        lax.all_to_all(moved[0], "seq", split_axis=1, concat_axis=2, tiled=True),
        lax.all_to_all(moved[1], "seq", split_axis=1, concat_axis=2, tiled=True),
        lax.all_to_all(moved[2], "seq", split_axis=1, concat_axis=2, tiled=True),
    )


def bring_back(relaid, block_masks, inverse):
    outputs = temporal_heads(relaid, block_masks)
    returned = lax.all_to_all(outputs, "seq", split_axis=2, concat_axis=1, tiled=True)
    restored = jnp.take(returned, inverse, axis=1)
    return jnp.swapaxes(restored, 1, 2)


def spatial_heads(query_heads, key_heads, value_heads, spatial_index, block_masks):

    def picked(tensor):
        return jnp.take(tensor, spatial_index, axis=0)

    return per_head(picked(query_heads), picked(key_heads), picked(value_heads), block_masks)


def shards(
    query_proj,
    key_proj,
    value_proj,
    query_gain,
    key_gain,
    head_class,
    spatial_mask,
    temporal_mask,
    location_order,
):
    token_count = query_proj.shape[0]
    head_count = head_class.shape[0]
    frame_count = token_count // LOCATIONS
    query_squares = jnp.sum(jnp.square(query_proj.astype(jnp.float32)), axis=1)
    key_squares = jnp.sum(jnp.square(key_proj.astype(jnp.float32)), axis=1)
    query_sums, key_sums = lax.psum((query_squares, key_squares), "head")

    def heads_major(tensor):
        return jnp.transpose(
            tensor.reshape(frame_count, LOCATIONS, head_count, HEAD_DIM), (2, 0, 1, 3)
        )

    query_heads = heads_major(normalize(query_proj, query_gain, query_sums))
    key_heads = heads_major(normalize(key_proj, key_gain, key_sums))
    value_heads = heads_major(value_proj)
    inverse = (
        jnp.zeros((LOCATIONS,), jnp.int32)
        .at[location_order]
        .set(jnp.arange(LOCATIONS, dtype=jnp.int32))
    )
    head_rank = jnp.argsort(1 - head_class, stable=True)
    moving = head_count * TEMPORAL // GROUP
    temporal_index = head_rank[:moving]
    spatial_index = head_rank[moving:]
    temporal_masks = jnp.take(temporal_mask, temporal_index, axis=0)
    spatial_masks = jnp.take(spatial_mask, spatial_index, axis=0)
    relaid = send_out(query_heads, key_heads, value_heads, temporal_index, location_order)
    temporal_out = bring_back(relaid, temporal_masks, inverse)
    spatial_out = spatial_heads(query_heads, key_heads, value_heads, spatial_index, spatial_masks)
    joined = jnp.concatenate([temporal_out, spatial_out], axis=0)
    placing = jnp.argsort(head_rank)
    placed = jnp.take(joined, placing, axis=0)
    return jnp.transpose(placed, (1, 2, 0, 3)).reshape(token_count, head_count * HEAD_DIM)


def solution(mesh):
    return jax.shard_map(
        shards,
        mesh=mesh,
        in_specs=(
            P("seq", "head"),
            P("seq", "head"),
            P("seq", "head"),
            P("head"),
            P("head"),
            P("head"),
            P("head", None, None),
            P("head", None, None),
            P(),
        ),
        out_specs=P("seq", "head"),
        check_vma=False,
    )
```

profile of v0, /device:TPU:98, one launch (start us, length us, event | category | flops | bytes accessed | tf_op | source)
XLA Modules:
  0.0 489.7 jit_solution(11618745014484523467)
XLA Ops:
  6.2 21.6 %all-reduce = (f32[3072]{0:T(1024)S(1)}, f32[3072]{0:T(1024)S(1)}) all-reduce(f32[3072]{0:T(1024)S(1)} %fusion.54, f32[3072]{0:T(1024)S(1)} %fusion.57), channel_id=1, replica_groups=mesh['seq'=16,'head'=8] {'head'}, use_global_device_ids=true, to_apply=%region_3.0 | all-reduce | flops 6144 | bytes 49152 | tf_op jit(solution)/shard_map/psum | solution.py:116
  32.1 9.5 %reshape.315 = bf16[2,1536,5,128]{3,2,1,0:T(8,128)(2,1)} reshape(bf16[3072,640]{1,0:T(8,128)(2,1)} %fusion.56) | data formatting | bytes 7864320 | tf_op jit(solution)/shard_map/reshape | solution.py:120
  49.9 9.5 %reshape.316 = bf16[2,1536,5,128]{3,2,1,0:T(8,128)(2,1)} reshape(bf16[3072,640]{1,0:T(8,128)(2,1)} %fusion.59) | data formatting | bytes 7864320 | tf_op jit(solution)/shard_map/reshape | solution.py:120
  64.8 9.5 %reshape.317 = bf16[2,1536,5,128]{3,2,1,0:T(8,128)(2,1)} reshape(bf16[3072,640]{1,0:T(8,128)(2,1)} %param.19) | data formatting | bytes 7864320 | tf_op jit(solution)/shard_map/reshape | solution.py:120
  98.1 13.5 %copy.93 = bf16[4,1536,2,128]{3,0,2,1:T(4,128)(2,1)} copy(bf16[4,1536,2,128]{3,1,2,0:T(8,128)(2,1)S(1)} %get-tuple-element.106) | data formatting | bytes 6291456 | tf_op jit(solution)/shard_map/transpose | solution.py:74
  111.7 13.1 %copy.89 = bf16[4,1536,2,128]{3,0,2,1:T(4,128)(2,1)} copy(bf16[4,1536,2,128]{3,1,2,0:T(8,128)(2,1)S(1)} %get-tuple-element.107) | data formatting | bytes 6291456 | tf_op jit(solution)/shard_map/transpose | solution.py:74
  124.8 10.0 %gather_fusion.7 = bf16[1536,4,2,128]{3,1,2,0:T(4,128)(2,1)S(1)} fusion(bf16[4,1536,2,128]{3,0,2,1:T(4,128)(2,1)} %copy.93, s32[2048]{0:T(1024)S(1)} %pad_clamp_fusion.1), kind=kCustom, calls=%fused_computation.5.clone | custom fusion | bytes 6297600 | tf_op jit(solution)/shard_map/jit(_take)/gather | solution.py:75
  134.8 9.8 %gather_fusion.5 = bf16[1536,4,2,128]{3,1,2,0:T(4,128)(2,1)} fusion(bf16[4,1536,2,128]{3,0,2,1:T(4,128)(2,1)} %copy.89, s32[2048]{0:T(1024)S(1)} %pad_clamp_fusion.1), kind=kCustom, calls=%fused_computation.4.clone | custom fusion | bytes 6297600 | tf_op jit(solution)/shard_map/jit(_take)/gather | solution.py:75
  144.6 6.3 %copy.85 = bf16[4,1536,2,128]{3,0,2,1:T(4,128)(2,1)} copy(bf16[4,1536,2,128]{3,1,2,0:T(8,128)(2,1)} %get-tuple-element.108) | data formatting | bytes 6291456 | tf_op jit(solution)/shard_map/transpose | solution.py:74
  150.9 9.7 %gather_fusion.3 = bf16[1536,4,2,128]{3,1,2,0:T(4,128)(2,1)} fusion(bf16[4,1536,2,128]{3,0,2,1:T(4,128)(2,1)} %copy.85, s32[2048]{0:T(1024)S(1)} %pad_clamp_fusion.1), kind=kCustom, calls=%fused_computation.1.clone | custom fusion | bytes 6297600 | tf_op jit(solution)/shard_map/jit(_take)/gather | solution.py:75
  160.5 9.3 %select_bitcast_fusion.2 = (bf16[4,1536,2,128]{3,0,2,1:T(4,128)(2,1)}, bf16[4,1536,2,128]{3,0,2,1:T(4,128)(2,1)S(1)}, bf16[4,1536,2,128]{3,0,2,1:T(4,128)(2,1)S(1)}) fusion(bf16[1536,4,2,128]{3,1,2,0:T(4,128)(2,1)S(1)} %gather_fusion.7, pred[1536]{0:T(1024)(128)(4,1)S(1)} %compare_and_fusion.1, bf16[1536,4,2,128]{3,1,2,0:T(4,128)(2,1)} %gather_fusion.5, ...), kind=kLoop, calls=%fused_computation.71 | loop fusion | flops 4718592 | bytes 18875904 | tf_op jit(solution)/shard_map/jit(_take)/select_n | solution.py:75
  169.8 46.7 %all_to_all.63 = bf16[4,1536,2,128]{3,0,2,1:T(4,128)(2,1)} all-to-all(bf16[4,1536,2,128]{3,0,2,1:T(4,128)(2,1)S(1)} %get-tuple-element.105), channel_id=1, replica_groups=mesh['seq'=16,'head'=8] {'seq'}, dimensions={1} | all-to-all | bytes 6291456 | tf_op jit(solution)/shard_map/all_to_all | solution.py:79
  216.5 43.4 %all_to_all.64 = bf16[4,1536,2,128]{3,0,2,1:T(4,128)(2,1)} all-to-all(bf16[4,1536,2,128]{3,0,2,1:T(4,128)(2,1)S(1)} %get-tuple-element.104), channel_id=1, replica_groups=mesh['seq'=16,'head'=8] {'seq'}, dimensions={1} | all-to-all | bytes 6291456 | tf_op jit(solution)/shard_map/all_to_all | solution.py:80
  279.4 6.2 %copy.86 = bf16[4,96,16,2,128]{4,3,2,1,0:T(2,128)(2,1)} copy(bf16[4,96,16,2,128]{4,0,3,1,2:T(4,128)(2,1)} %bitcast.160) | data formatting | bytes 6291456 | tf_op jit(solution)/shard_map/all_to_all | solution.py:79
  289.6 14.4 %all-to-all-done.2 = bf16[4,1536,2,128]{3,0,2,1:T(4,128)(2,1)S(1)} async-done(((bf16[4,1536,2,128]{3,0,2,1:T(4,128)(2,1)}), bf16[4,1536,2,128]{3,0,2,1:T(4,128)(2,1)S(1)}, u32[]{:S(2)}, u32[]{:S(2)}) %all-to-all-start.2) | async-done | bytes 3145760 | tf_op jit(solution)/shard_map/all_to_all | solution.py:81
  308.1 64.5 %while.16 = (s32[]{:T(128)}, bf16[4,3,1024,128]{3,2,1,0:T(8,128)(2,1)}, s32[4,8,8]{2,1,0:T(8,128)S(1)}, bf16[4,3,1024,128]{3,2,1,0:T(8,128)(2,1)}, bf16[4,3,1024...) while((s32[]{:T(128)}, bf16[4,3,1024,128]{3,2,1,0:T(8,128)(2,1)}, ...), condition=%wide.region_9.12_spmd, body=%wide.region_6.11_spmd.sunk | while | flops 1630274816 | bytes 20998744 | solution.py:55
  309.5 8.8 %fusion.131 = (f32[3,1024]{1,0:T(4,128)S(1)}, bf16[3,1024,1024]{1,2,0:T(8,128)(2,1)}) fusion(pred[1024,1024]{0,1:T(8,128)(4,1)S(1)} %bitcast.150, bf16[4,3,1024,128]{3,2,1,0:T(8,128)(2,1)} %get-tuple-element.176, s32[]{:T(128)S(6)} %copy.138, bf16[4,3,1024,128]{3,2,1,0:T(8,128)(2,1)} %get-tuple-element.175), kind=kOutput, calls=%fused_computation.126.clone.1 | convolution fusion | flops 824181760 | bytes 9974784 | tf_op jit(solution)/shard_map/while/body/eval_jaxpr/sub | solution.py:35
  318.3 6.2 %fusion.132 = bf16[4,3,1024,128]{3,2,1,0:T(8,128)(2,1)} fusion(bf16[4,3,1024,128]{3,2,1,0:T(8,128)(2,1)} %get-tuple-element.166, s32[]{:T(128)S(6)} %copy.138, bf16[3,1024,1024]{1,2,0:T(8,128)(2,1)} %get-tuple-element.156, f32[3,1024]{1,0:T(4,128)S(1)} %get-tuple-element.157, bf16[4,3,1024,128]{3,2,1,0:T(8,128)(2,1)} %get-tuple-element.177), kind=kOutput, calls=%fused_computation.23.clone.1 | convolution fusion | flops 806092800 | bytes 7877632 | tf_op jit(solution)/shard_map/while/body/eval_jaxpr/gqk,gkd->gqd/dot_general | solution.py:37
  325.5 8.8 %fusion.131 = (f32[3,1024]{1,0:T(4,128)S(1)}, bf16[3,1024,1024]{1,2,0:T(8,128)(2,1)}) fusion(pred[1024,1024]{0,1:T(8,128)(4,1)S(1)} %bitcast.150, bf16[4,3,1024,128]{3,2,1,0:T(8,128)(2,1)} %get-tuple-element.176, s32[]{:T(128)S(6)} %copy.138, bf16[4,3,1024,128]{3,2,1,0:T(8,128)(2,1)} %get-tuple-element.175), kind=kOutput, calls=%fused_computation.126.clone.1 | convolution fusion | flops 824181760 | bytes 9974784 | tf_op jit(solution)/shard_map/while/body/eval_jaxpr/sub | solution.py:35
  334.3 6.2 %fusion.132 = bf16[4,3,1024,128]{3,2,1,0:T(8,128)(2,1)} fusion(bf16[4,3,1024,128]{3,2,1,0:T(8,128)(2,1)} %get-tuple-element.166, s32[]{:T(128)S(6)} %copy.138, bf16[3,1024,1024]{1,2,0:T(8,128)(2,1)} %get-tuple-element.156, f32[3,1024]{1,0:T(4,128)S(1)} %get-tuple-element.157, bf16[4,3,1024,128]{3,2,1,0:T(8,128)(2,1)} %get-tuple-element.177), kind=kOutput, calls=%fused_computation.23.clone.1 | convolution fusion | flops 806092800 | bytes 7877632 | tf_op jit(solution)/shard_map/while/body/eval_jaxpr/gqk,gkd->gqd/dot_general | solution.py:37
  341.5 8.8 %fusion.131 = (f32[3,1024]{1,0:T(4,128)S(1)}, bf16[3,1024,1024]{1,2,0:T(8,128)(2,1)}) fusion(pred[1024,1024]{0,1:T(8,128)(4,1)S(1)} %bitcast.150, bf16[4,3,1024,128]{3,2,1,0:T(8,128)(2,1)} %get-tuple-element.176, s32[]{:T(128)S(6)} %copy.138, bf16[4,3,1024,128]{3,2,1,0:T(8,128)(2,1)} %get-tuple-element.175), kind=kOutput, calls=%fused_computation.126.clone.1 | convolution fusion | flops 824181760 | bytes 9974784 | tf_op jit(solution)/shard_map/while/body/eval_jaxpr/sub | solution.py:35
  350.3 6.2 %fusion.132 = bf16[4,3,1024,128]{3,2,1,0:T(8,128)(2,1)} fusion(bf16[4,3,1024,128]{3,2,1,0:T(8,128)(2,1)} %get-tuple-element.166, s32[]{:T(128)S(6)} %copy.138, bf16[3,1024,1024]{1,2,0:T(8,128)(2,1)} %get-tuple-element.156, f32[3,1024]{1,0:T(4,128)S(1)} %get-tuple-element.157, bf16[4,3,1024,128]{3,2,1,0:T(8,128)(2,1)} %get-tuple-element.177), kind=kOutput, calls=%fused_computation.23.clone.1 | convolution fusion | flops 806092800 | bytes 7877632 | tf_op jit(solution)/shard_map/while/body/eval_jaxpr/gqk,gkd->gqd/dot_general | solution.py:37
  357.6 8.8 %fusion.131 = (f32[3,1024]{1,0:T(4,128)S(1)}, bf16[3,1024,1024]{1,2,0:T(8,128)(2,1)}) fusion(pred[1024,1024]{0,1:T(8,128)(4,1)S(1)} %bitcast.150, bf16[4,3,1024,128]{3,2,1,0:T(8,128)(2,1)} %get-tuple-element.176, s32[]{:T(128)S(6)} %copy.138, bf16[4,3,1024,128]{3,2,1,0:T(8,128)(2,1)} %get-tuple-element.175), kind=kOutput, calls=%fused_computation.126.clone.1 | convolution fusion | flops 824181760 | bytes 9974784 | tf_op jit(solution)/shard_map/while/body/eval_jaxpr/sub | solution.py:35
  366.4 6.2 %fusion.132 = bf16[4,3,1024,128]{3,2,1,0:T(8,128)(2,1)} fusion(bf16[4,3,1024,128]{3,2,1,0:T(8,128)(2,1)} %get-tuple-element.166, s32[]{:T(128)S(6)} %copy.138, bf16[3,1024,1024]{1,2,0:T(8,128)(2,1)} %get-tuple-element.156, f32[3,1024]{1,0:T(4,128)S(1)} %get-tuple-element.157, bf16[4,3,1024,128]{3,2,1,0:T(8,128)(2,1)} %get-tuple-element.177), kind=kOutput, calls=%fused_computation.23.clone.1 | convolution fusion | flops 806092800 | bytes 7877632 | tf_op jit(solution)/shard_map/while/body/eval_jaxpr/gqk,gkd->gqd/dot_general | solution.py:37
  377.3 7.7 %all-to-all-start.3 = ((bf16[4,96,32,128]{3,1,0,2:T(8,128)(2,1)}), bf16[4,96,32,128]{3,1,0,2:T(8,128)(2,1)S(1)}, u32[]{:S(2)}, u32[]{:S(2)}) async-start(bf16[4,96,32,128]{3,1,0,2:T(8,128)(2,1)} %copy.95), calls=%async_computation.3 | async-start | bytes 6291456 | tf_op jit(solution)/shard_map/all_to_all | solution.py:87
  385.1 14.4 %fusion.112 = (f32[2,1536]{1,0:T(2,128)S(1)}, bf16[2,1536,1536]{1,2,0:T(8,128)(2,1)}) fusion(pred[1536,1536]{0,1:T(8,128)(4,1)} %copy.99, bf16[5,2,1536,128]{3,2,1,0:T(8,128)(2,1)} %bitcast.153, s32[]{:T(128)} %bitcast.31, pred[]{:T(512)} %bitcast.30, bf16[5,2,1536,128]{3,2,1,0:T(8,128)(2,1)} %bitcast.157), kind=kOutput, calls=%fused_computation.127 | convolution fusion | flops 1237059072 | bytes 15742976 | tf_op jit(solution)/shard_map/while/body/eval_jaxpr/sub | solution.py:35
  399.4 7.7 %fusion.68 = bf16[1,2,1536,128]{3,2,1,0:T(8,128)(2,1)S(1)} fusion(bf16[2,1536,1536]{1,2,0:T(8,128)(2,1)} %get-tuple-element.110, bf16[5,2,1536,128]{3,2,1,0:T(8,128)(2,1)} %bitcast.155, s32[]{:T(128)} %bitcast.31, f32[2,1536]{1,0:T(2,128)S(1)} %get-tuple-element.109, pred[]{:T(512)} %bitcast.30), kind=kOutput, calls=%fused_computation.80 | convolution fusion | flops 1209139200 | bytes 11023360 | tf_op jit(solution)/shard_map/while/body/eval_jaxpr/gqk,gkd->gqd/dot_general | solution.py:37
  407.1 9.9 %copy.101 = bf16[1,2,1536,128]{3,0,1,2:T(2,128)(2,1)} copy(bf16[1,2,1536,128]{3,2,1,0:T(8,128)(2,1)S(1)} %fusion.68) | data formatting | bytes 1572864 | tf_op jit(solution)/shard_map/while/body/jit(dynamic_update_index_in_dim)/broadcast_in_dim | solution.py:55
  417.1 6.2 %scatter_custom_fusion = s32[1536]{0:T(1024)S(1)} fusion(s32[1536]{0:T(1024)S(1)} %compare_select_fusion.1, s32[1536]{0:T(1024)S(1)} %iota.45, s32[]{:T(128)} %constant.96.clone.1), kind=kCustom, calls=%fused_computation.111 | custom fusion | bytes 6148 | tf_op jit(solution)/shard_map/scatter | solution.py:129
  424.6 13.3 %copy.98 = bf16[4,1536,2,128]{3,0,2,1:T(4,128)(2,1)} copy(bf16[4,1536,2,128]{3,1,2,0:T(8,128)(2,1)S(1)} %bitcast.162) | data formatting | bytes 6291456 | tf_op jit(solution)/shard_map/all_to_all | solution.py:87
  437.9 10.0 %gather_fusion.8 = bf16[1536,4,2,128]{3,1,2,0:T(4,128)(2,1)S(1)} fusion(bf16[4,1536,2,128]{3,0,2,1:T(4,128)(2,1)} %copy.98, s32[2048]{0:T(1024)S(1)} %pad_clamp_fusion), kind=kCustom, calls=%fused_computation.6.clone | custom fusion | bytes 6297600 | tf_op jit(solution)/shard_map/jit(_take)/gather | solution.py:88
  467.9 18.5 %copy.114 = bf16[2,1536,5,128]{3,2,1,0:T(8,128)(2,1)S(1)} copy(bf16[2,1536,5,128]{3,1,0,2:T(8,128)(2,1)S(1)} %select_bitcast_fusion) | data formatting | bytes 7864320 | tf_op jit(solution)/shard_map/reshape | solution.py:143
  (81 shorter events, 106.3 us)
Async XLA Ops:
  0.0 278.7 %copy-start = (s32[5,8,8]{2,1,0:T(8,128)S(1)}, s32[5,8,8]{2,1,0:T(8,128)}, u32[]{:S(2)}) copy-start(s32[5,8,8]{2,1,0:T(8,128)} %param.24) | copy-start | bytes 3844
  0.0 5.4 %copy-start.2 = (bf16[3072,640]{1,0:T(8,128)(2,1)S(1)}, bf16[3072,640]{1,0:T(8,128)(2,1)}, u32[]{:S(2)}) copy-start(bf16[3072,640]{1,0:T(8,128)(2,1)} %param.18) | copy-start | bytes 11796484
  2.4 25.4 %copy-start.6 = (f32[640]{0:T(1024)S(1)}, f32[640]{0:T(1024)}, u32[]{:S(2)}) copy-start(f32[640]{0:T(1024)} %param.20) | copy-start | bytes 7684
  41.6 5.5 %copy-start.3 = (bf16[3072,640]{1,0:T(8,128)(2,1)S(1)}, bf16[3072,640]{1,0:T(8,128)(2,1)}, u32[]{:S(2)}) copy-start(bf16[3072,640]{1,0:T(8,128)(2,1)} %param.18) | copy-start | bytes 11796484
  41.6 5.5 %copy-start.7 = (f32[640]{0:T(1024)S(1)}, f32[640]{0:T(1024)}, u32[]{:S(2)}) copy-start(f32[640]{0:T(1024)} %param.21) | copy-start | bytes 7684
  259.9 44.0 %all-to-all-start.2 = ((bf16[4,1536,2,128]{3,0,2,1:T(4,128)(2,1)}), bf16[4,1536,2,128]{3,0,2,1:T(4,128)(2,1)S(1)}, u32[]{:S(2)}, u32[]{:S(2)}) async-start(bf16[4,1536,2,128]{3,0,2,1:T(4,128)(2,1)} %get-tuple-element.103), calls=%async_computation.2 | async-start | bytes 6291456 | tf_op jit(solution)/shard_map/all_to_all | solution.py:81
  279.4 6.2 %copy-start.4 = (bf16[4,1536,2,128]{3,0,2,1:T(4,128)(2,1)S(1)}, bf16[4,1536,2,128]{3,0,2,1:T(4,128)(2,1)}, u32[]{:S(2)}) copy-start(bf16[4,1536,2,128]{3,0,2,1:T(4,128)(2,1)} %all_to_all.64) | copy-start | bytes 9437188
  377.3 47.0 %all-to-all-start.3 = ((bf16[4,96,32,128]{3,1,0,2:T(8,128)(2,1)}), bf16[4,96,32,128]{3,1,0,2:T(8,128)(2,1)S(1)}, u32[]{:S(2)}, u32[]{:S(2)}) async-start(bf16[4,96,32,128]{3,1,0,2:T(8,128)(2,1)} %copy.95), calls=%async_computation.3 | async-start | bytes 6291456 | tf_op jit(solution)/shard_map/all_to_all | solution.py:87
  447.9 5.7 %copy-start.5 = (bf16[1,2,1536,128]{3,0,1,2:T(2,128)(2,1)S(1)}, bf16[1,2,1536,128]{3,0,1,2:T(2,128)(2,1)}, u32[]{:S(2)}) copy-start(bf16[1,2,1536,128]{3,0,1,2:T(2,128)(2,1)} %copy.101) | copy-start | bytes 2359300
  486.4 2.9 copy-start.1
where the time goes:
time: 499 us; the launch traced here: 490 us
  local copies, waits for them, and re-layouts  223 us (45%)
  blocking collectives  112 us (22%)
  matrix products  82.3 us (16%)
  other arithmetic  41.6 us (8%)
  waiting for transfers between devices  14.4 us (3%)
  starting transfers between devices  13.7 us (3%)
    sub x5, matrix products, attend(): weights = jnp.where(allowed, jnp.exp(scores - row_top), 0.0)  49.8 us
    all_to_all x1, blocking collectives, send_out(): lax.all_to_all(moved[0], 'seq', split_axis=1, concat_axis=2, tiled=True)  46.7 us
    reshape x6, local copies, waits for them, and re-layouts, heads_major(): tensor.reshape(frame_count, LOCATIONS, head_count, HEAD_DIM)  44.8 us
    all_to_all x1, blocking collectives, send_out(): lax.all_to_all(moved[1], 'seq', split_axis=1, concat_axis=2, tiled=True)  43.4 us
    transpose x3, local copies, waits for them, and re-layouts, location_major(): turned = jnp.swapaxes(picked, 1, 2)  32.9 us
    dot_general x5, matrix products, attend(): jnp.einsum('gqk,gkd->gqd', weights.astype(jnp.bfloat16), values, preferre...  32.5 us
    gather x3, local copies, waits for them, and re-layouts, location_major(): return jnp.take(turned, location_order, axis=1)  29.5 us
    psum x1, blocking collectives, shards(): query_sums, key_sums = lax.psum((query_squares, key_squares), 'head')  21.6 us
  transfers between devices with their start and end apart: 2, of which 1 were waited for; matrix products, arithmetic and copies ran while one was open for 12% of the time, Pallas kernels for 0%

commit v1 on v0

v1 whole, which is shorter than its diff:
```python
import functools

import jax
import jax.numpy as jnp
from jax import lax
from jax.experimental import pallas as pl
from jax.experimental.pallas import tpu as pltpu
from jax.sharding import PartitionSpec as P

HEADS = 40
HEAD_DIM = 128
LOCATIONS = 1536
BLOCK = 128
WINDOW_SPAN = 32
GROUP = 5
TEMPORAL = 4
FEATURES = HEADS * HEAD_DIM
EPSILON = 1e-06
MASKED = -1e30
EXP2_SCALE = 1.4426950408889634 * HEAD_DIM ** (-0.5)
LANE_BLOCKS = LOCATIONS // 128
VMEM_LIMIT = 40 * 2**20

F32 = jnp.float32
BF16 = jnp.bfloat16


def params(vmem=VMEM_LIMIT):
    return pltpu.CompilerParams(vmem_limit_bytes=vmem)


def cost(flops, nbytes, exps=0):
    return pl.CostEstimate(flops=int(flops), bytes_accessed=int(nbytes), transcendentals=int(exps))


def spatial_head(class_ref):
    found = jnp.int32(0)
    for i in range(1, GROUP):
        found = found + i * (1 - class_ref[i])
    return found


def temporal_head(class_ref, j):
    return j + (j >= spatial_head(class_ref)).astype(jnp.int32)


def column(row):
    return jnp.broadcast_to(row, (128, 128)).T


def sums_kernel(q_ref, k_ref, out_ref):
    for a, ref in enumerate((q_ref, k_ref)):
        for i in range(q_ref.shape[0] // 128):
            part = jnp.zeros((128, 128), F32)
            for j in range(GROUP):
                x = ref[128 * i : 128 * i + 128, 128 * j : 128 * j + 128].astype(F32)
                part = part + x * x
            out_ref[a, 0, i, :] = jnp.sum(part.T, axis=0)


def square_sums(query_proj, key_proj):
    tokens, features = query_proj.shape
    frames = tokens // LOCATIONS
    in_spec = pl.BlockSpec((LOCATIONS, features), lambda f: (f, 0))
    return pl.pallas_call(
        sums_kernel,
        grid=(frames,),
        in_specs=[in_spec, in_spec],
        out_specs=pl.BlockSpec((2, 1, LANE_BLOCKS, 128), lambda f: (0, f, 0, 0)),
        out_shape=jax.ShapeDtypeStruct((2, frames, LANE_BLOCKS, 128), F32),
        compiler_params=params(),
        cost_estimate=cost(4 * tokens * features, 4 * tokens * features),
        name="square_sums",
    )(query_proj, key_proj)


def build_picked(order_ref, picked_ref):
    lanes = lax.broadcasted_iota(jnp.int32, (128, 128), 1).astype(F32)
    for i in range(LANE_BLOCKS):
        wanted = column(order_ref[i : i + 1, :].astype(F32))
        for j in range(LANE_BLOCKS):
            hit = wanted == lanes + float(128 * j)
            picked_ref[128 * i : 128 * i + 128, 128 * j : 128 * j + 128] = jnp.where(
                hit, 1.0, 0.0
            ).astype(BF16)


def pick_rows(picked_ref, heads_ref, store):
    rows = 384
    for c in range(LOCATIONS // rows):
        y = jnp.dot(
            picked_ref[rows * c : rows * c + rows, :],
            heads_ref[...],
            preferred_element_type=F32,
        ).astype(BF16)
        store(c, rows, y)


def pack_value_kernel(class_ref, order_ref, x_ref, out_ref, picked_ref, heads_ref):
    @pl.when(pl.program_id(0) == 0)
    def _():
        build_picked(order_ref, picked_ref)

    for j in range(TEMPORAL):
        h = temporal_head(class_ref, j)
        heads_ref[:, 128 * j : 128 * j + 128] = x_ref[
            :, pl.ds(pl.multiple_of(h * 128, 128), 128)
        ]

    def store(c, rows, y):
        slots = rows // 96
        for j in range(TEMPORAL):
            out_ref[slots * c : slots * c + slots, j, 0] = y[
                :, 128 * j : 128 * j + 128
            ].reshape(slots, 96, 128)

    pick_rows(picked_ref, heads_ref, store)


def pack_values(value_proj, head_class, order):
    tokens, features = value_proj.shape
    frames = tokens // LOCATIONS
    return pl.pallas_call(
        pack_value_kernel,
        grid_spec=pltpu.PrefetchScalarGridSpec(
            num_scalar_prefetch=1,
            grid=(frames,),
            in_specs=[
                pl.BlockSpec((LANE_BLOCKS, 128), lambda f, c: (0, 0)),
                pl.BlockSpec((LOCATIONS, features), lambda f, c: (f, 0)),
            ],
            out_specs=pl.BlockSpec((16, TEMPORAL, 1, 96, 128), lambda f, c: (0, 0, f, 0, 0)),
            scratch_shapes=[
                pltpu.VMEM((LOCATIONS, LOCATIONS), BF16),
                pltpu.VMEM((LOCATIONS, TEMPORAL * 128), BF16),
            ],
        ),
        out_shape=jax.ShapeDtypeStruct((16, TEMPORAL, frames, 96, 128), BF16),
        compiler_params=params(),
        cost_estimate=cost(2 * tokens * LOCATIONS * 512, 4 * tokens * features),
        name="pack_values",
    )(head_class, order, value_proj)


def factor_of(sums):
    return lax.rsqrt(sums * (1.0 / FEATURES) + EPSILON)


def pack_norm_kernel(
    split, class_ref, order_ref, sums_ref, gain_ref, q_ref, k_ref, *rest
):
    out_refs, (picked_ref, heads_ref) = rest[:-2], rest[-2:]

    @pl.when((pl.program_id(0) == 0) & (pl.program_id(1) == 0))
    def _():
        build_picked(order_ref, picked_ref)

    def load(x_ref):
        factor = factor_of(sums_ref[0, 0])
        for i in range(LANE_BLOCKS):
            scale = column(factor[i : i + 1, :])
            for j in range(TEMPORAL):
                h = pl.multiple_of(temporal_head(class_ref, j) * 128, 128)
                x = x_ref[128 * i : 128 * i + 128, pl.ds(h, 128)].astype(F32)
                gain = gain_ref[0, :, pl.ds(h, 128)]
                heads_ref[128 * i : 128 * i + 128, 128 * j : 128 * j + 128] = (
                    x * scale * gain
                ).astype(BF16)

    @pl.when(pl.program_id(0) == 0)
    def _():
        load(q_ref)

    @pl.when(pl.program_id(0) == 1)
    def _():
        load(k_ref)

    def store(c, rows, y):
        slots = rows // 96
        j = 0
        for out_ref, count in zip(out_refs, split):
            for i in range(count):
                out_ref[slots * c : slots * c + slots, i, 0, 0] = y[
                    :, 128 * j : 128 * j + 128
                ].reshape(slots, 96, 128)
                j += 1

    pick_rows(picked_ref, heads_ref, store)


def pack_norms(query_proj, key_proj, sums, gains, head_class, order, split):
    tokens, features = query_proj.shape
    frames = tokens // LOCATIONS
    return pl.pallas_call(
        functools.partial(pack_norm_kernel, split),
        grid_spec=pltpu.PrefetchScalarGridSpec(
            num_scalar_prefetch=1,
            grid=(2, frames),
            in_specs=[
                pl.BlockSpec((LANE_BLOCKS, 128), lambda a, f, c: (0, 0)),
                pl.BlockSpec((1, 1, LANE_BLOCKS, 128), lambda a, f, c: (a, f, 0, 0)),
                pl.BlockSpec((1, 1, features), lambda a, f, c: (a, 0, 0)),
                pl.BlockSpec((LOCATIONS, features), lambda a, f, c: (f * (1 - a) + a * (frames - 1), 0)),
                pl.BlockSpec((LOCATIONS, features), lambda a, f, c: (f * a, 0)),
            ],
            out_specs=[
                pl.BlockSpec((16, n, 1, 1, 96, 128), lambda a, f, c: (0, 0, a, f, 0, 0))
                for n in split
            ],
            scratch_shapes=[
                pltpu.VMEM((LOCATIONS, LOCATIONS), BF16),
                pltpu.VMEM((LOCATIONS, TEMPORAL * 128), BF16),
            ],
        ),
        out_shape=[jax.ShapeDtypeStruct((16, n, 2, frames, 96, 128), BF16) for n in split],
        compiler_params=params(),
        cost_estimate=cost(4 * tokens * LOCATIONS * 512, 8 * tokens * features),
        name="pack_norms",
    )(head_class, order, sums, gains, query_proj, key_proj)


def softmax_rows(queries, key_rows, values, bias):
    s = lax.dot_general(
        queries, key_rows, (((1,), (1,)), ((), ())), preferred_element_type=F32
    )
    rows, keys = s.shape
    s = (s.reshape(-1, *bias.shape) + bias).reshape(rows, keys)
    top = jnp.max(s, axis=1, keepdims=True)
    w = jnp.exp2((s - top) * EXP2_SCALE)
    total = jnp.sum(w, axis=1, keepdims=True)
    mixture = jnp.dot(w.astype(BF16), values, preferred_element_type=F32)
    return (mixture / total).astype(BF16)


def window_kernel(class_ref, bias_ref, q_ref, k_ref, v_ref, *rest):
    out_ref = rest[-1]
    tokens = 16 * 2 * WINDOW_SPAN
    q = q_ref[...].reshape(tokens, 128)
    k = k_ref[...].reshape(tokens, 128)
    v = v_ref[...].reshape(tokens, 128)
    bias = bias_ref[0]
    rows = 256
    for c in range(tokens // rows):
        o = softmax_rows(q[rows * c : rows * c + rows], k, v, bias)
        slots = rows // (2 * WINDOW_SPAN)
        out_ref[slots * c : slots * c + slots, 0] = o.reshape(slots, 2, WINDOW_SPAN, 128)


def window_attention(moved, values, bias, head_class, first, before):
    count = moved.shape[1]
    windows = 96 // WINDOW_SPAN
    block = (16, 1, 2, WINDOW_SPAN, 128)
    qk_block = (16, 1, 1, 2, WINDOW_SPAN, 128)
    in_specs = [
        pl.BlockSpec(
            (1, WINDOW_SPAN, 1024), lambda h, w, c: (temporal_head(c, h + first), 0, 0)
        ),
        pl.BlockSpec(qk_block, lambda h, w, c: (0, h, 0, 0, w, 0)),
        pl.BlockSpec(qk_block, lambda h, w, c: (0, h, 1, 0, w, 0)),
        pl.BlockSpec(block, lambda h, w, c: (0, h + first, 0, w, 0)),
    ]
    operands = [head_class, bias, moved, moved, values]
    aliases = {}
    if before is not None:
        in_specs.append(pl.BlockSpec(memory_space=pl.ANY))
        aliases = {len(operands): 0}
        operands.append(before)
    return pl.pallas_call(
        window_kernel,
        grid_spec=pltpu.PrefetchScalarGridSpec(
            num_scalar_prefetch=1,
            grid=(count, windows),
            in_specs=in_specs,
            out_specs=pl.BlockSpec(block, lambda h, w, c: (0, h + first, 0, w, 0)),
        ),
        out_shape=jax.ShapeDtypeStruct((16, TEMPORAL, 2, 96, 128), BF16),
        input_output_aliases=aliases,
        compiler_params=params(),
        cost_estimate=cost(
            8 * count * windows * 1024 * 1024 * 128, 8 * count * windows * 1024 * 128, count * windows * 1024 * 1024
        ),
        name="window_attention",
    )(*operands)


def frame_kernel(class_ref, bias_ref, sums_ref, gain_ref, q_ref, k_ref, v_ref, out_ref, qn_ref, kn_ref):
    for a, (x_ref, n_ref) in enumerate(((q_ref, qn_ref), (k_ref, kn_ref))):
        factor = factor_of(sums_ref[a, 0])
        for i in range(LANE_BLOCKS):
            x = x_ref[128 * i : 128 * i + 128, :].astype(F32)
            n_ref[128 * i : 128 * i + 128, :] = (
                x * column(factor[i : i + 1, :]) * gain_ref[a]
            ).astype(BF16)

    def body(i, carry):
        rows = pl.ds(pl.multiple_of(i * 128, 128), 128)
        out_ref[rows, :] = softmax_rows(
            qn_ref[rows, :], kn_ref[...], v_ref[...], bias_ref[0, pl.ds(i, 1), :]
        )
        return carry

    lax.fori_loop(0, LANE_BLOCKS, body, 0)


def frame_attention(query_proj, key_proj, value_proj, sums, gains, bias, head_class):
    tokens = query_proj.shape[0]
    frames = tokens // LOCATIONS
    column_spec = pl.BlockSpec((LOCATIONS, 128), lambda f, c: (f, spatial_head(c)))
    return pl.pallas_call(
        frame_kernel,
        grid_spec=pltpu.PrefetchScalarGridSpec(
            num_scalar_prefetch=1,
            grid=(frames,),
            in_specs=[
                pl.BlockSpec((1, LANE_BLOCKS, LOCATIONS), lambda f, c: (spatial_head(c), 0, 0)),
                pl.BlockSpec((2, 1, LANE_BLOCKS, 128), lambda f, c: (0, f, 0, 0)),
                pl.BlockSpec((2, 1, 128), lambda f, c: (0, 0, spatial_head(c))),
                column_spec,
                column_spec,
                column_spec,
            ],
            out_specs=pl.BlockSpec((LOCATIONS, 128), lambda f, c: (f, 0)),
            scratch_shapes=[
                pltpu.VMEM((LOCATIONS, 128), BF16),
                pltpu.VMEM((LOCATIONS, 128), BF16),
            ],
        ),
        out_shape=jax.ShapeDtypeStruct((tokens, 128), BF16),
        compiler_params=params(),
        cost_estimate=cost(
            4 * tokens * LOCATIONS * 256, 8 * tokens * 128, tokens * LOCATIONS
        ),
        name="frame_attention",
    )(head_class, bias, sums, gains, query_proj, key_proj, value_proj)


def unpack_kernel(class_ref, order_ref, spatial_ref, moved_ref, out_ref, heads_ref):
    rows = out_ref.shape[0]
    first = pl.program_id(1) * rows
    for j in range(TEMPORAL):
        heads_ref[:, 128 * j : 128 * j + 128] = moved_ref[:, j, 0].reshape(LOCATIONS, 128)
    places = lax.broadcasted_iota(jnp.int32, (rows, 128), 0) + first
    parts = []
    for i in range(LANE_BLOCKS):
        hit = order_ref[i : i + 1, :] == places
        parts.append(jnp.where(hit, 1.0, 0.0).astype(BF16))
    y = jnp.dot(
        jnp.concatenate(parts, axis=1), heads_ref[...], preferred_element_type=F32
    ).astype(BF16)
    for j in range(TEMPORAL):
        h = pl.multiple_of(temporal_head(class_ref, j) * 128, 128)
        out_ref[:, pl.ds(h, 128)] = y[:, 128 * j : 128 * j + 128]
    h = pl.multiple_of(spatial_head(class_ref) * 128, 128)
    out_ref[:, pl.ds(h, 128)] = spatial_ref[...]


def unpack(returned, spatial_out, head_class, order):
    frames = returned.shape[2]
    tokens = frames * LOCATIONS
    rows = 768
    steps = LOCATIONS // rows
    return pl.pallas_call(
        unpack_kernel,
        grid_spec=pltpu.PrefetchScalarGridSpec(
            num_scalar_prefetch=1,
            grid=(frames, steps),
            in_specs=[
                pl.BlockSpec((LANE_BLOCKS, 128), lambda f, i, c: (0, 0)),
                pl.BlockSpec((rows, 128), lambda f, i, c: (f * steps + i, 0)),
                pl.BlockSpec((16, TEMPORAL, 1, 96, 128), lambda f, i, c: (0, 0, f, 0, 0)),
            ],
            out_specs=pl.BlockSpec((rows, GROUP * 128), lambda f, i, c: (f * steps + i, 0)),
            scratch_shapes=[pltpu.VMEM((LOCATIONS, TEMPORAL * 128), BF16)],
        ),
        out_shape=jax.ShapeDtypeStruct((tokens, GROUP * 128), BF16),
        compiler_params=params(),
        cost_estimate=cost(2 * tokens * LOCATIONS * 512, 4 * tokens * 640),
        name="unpack",
    )(head_class, order, spatial_out, returned)


def spread_mask(mask, repeat):
    blocks = mask.shape[-1]
    same = jnp.arange(blocks)[:, None] == jnp.arange(blocks)[None, :]
    bias = jnp.where((mask != 0) | same, 0.0, MASKED).astype(F32)
    return jnp.repeat(bias, repeat, axis=2)


def exchange(tensor):
    return lax.all_to_all(tensor, "seq", split_axis=0, concat_axis=0, tiled=True)


SPLIT = (3, 1)


def shards(
    query_proj,
    key_proj,
    value_proj,
    query_gain,
    key_gain,
    head_class,
    spatial_mask,
    temporal_mask,
    location_order,
):
    order = location_order.reshape(LANE_BLOCKS, 128)
    gains = jnp.stack([query_gain, key_gain])[:, None, :]
    window_bias = jnp.tile(
        jnp.repeat(spread_mask(temporal_mask, 4), 4, axis=1), (1, 1, 32)
    )
    frame_bias = spread_mask(spatial_mask, 128)

    packed_values = pack_values(value_proj, head_class, order)
    sums = square_sums(query_proj, key_proj)
    values = exchange(packed_values)
    sums = lax.psum(sums, "head")
    packed = pack_norms(query_proj, key_proj, sums, gains, head_class, order, SPLIT)
    values, *packed = lax.optimization_barrier((values, *packed))

    moved = exchange(packed[0])
    spatial_out = frame_attention(
        query_proj, key_proj, value_proj, sums, gains, frame_bias, head_class
    )
    moved, spatial_out, later = lax.optimization_barrier((moved, spatial_out, packed[1]))

    moved_later = exchange(later)
    mixed = window_attention(moved, values, window_bias, head_class, 0, None)
    mixed, moved_later = lax.optimization_barrier((mixed, moved_later))

    mixed = window_attention(moved_later, values, window_bias, head_class, SPLIT[0], mixed)
    returned = exchange(mixed)
    return unpack(returned, spatial_out, head_class, order)


def solution(mesh):
    return jax.shard_map(
        shards,
        mesh=mesh,
        in_specs=(
            P("seq", "head"),
            P("seq", "head"),
            P("seq", "head"),
            P("head"),
            P("head"),
            P("head"),
            P("head", None, None),
            P("head", None, None),
            P(),
        ),
        out_specs=P("seq", "head"),
        check_vma=False,
    )
```

time: 499 us -> 252 us (0.51)
  the two profiles are of different devices: /device:TPU:98 before, /device:TPU:96 now
where the time goes in v1:
time: 252 us; the launch traced here: 251 us
  Pallas kernels  81.2 us (32%)
  blocking collectives  68.6 us (27%)
  local copies, waits for them, and re-layouts  35.9 us (14%)
  waiting for transfers between devices  35.8 us (14%)
  starting transfers between devices  29.5 us (12%)
    all_to_all x1, blocking collectives, exchange(): lax.all_to_all(tensor, 'seq', split_axis=0, concat_axis=0, tiled=True)  46.2 us
    all_to_all x3, waiting for transfers between devices, exchange(): lax.all_to_all(tensor, 'seq', split_axis=0, concat_axis=0, tiled=True)  35.8 us
    unnamed x46, local copies, waits for them, and re-layouts  31.1 us
    all_to_all x3, starting transfers between devices, exchange(): lax.all_to_all(tensor, 'seq', split_axis=0, concat_axis=0, tiled=True)  29.5 us
    pallas_call x2, Pallas kernels, window_attention(): pl.pallas_call(window_kernel, grid_spec=pltpu.PrefetchScalarGridSpec(num_...  27.4 us
    psum x1, blocking collectives, shards(): sums = lax.psum(sums, 'head')  22.3 us
    pallas_call x1, Pallas kernels, frame_attention(): pl.pallas_call(frame_kernel, grid_spec=pltpu.PrefetchScalarGridSpec(num_s...  21.8 us
    pallas_call x1, Pallas kernels, pack_norms(): pl.pallas_call(functools.partial(pack_norm_kernel, split), grid_spec=pltp...  15.1 us
  transfers between devices with their start and end apart: 3, of which 1 were waited for; matrix products, arithmetic and copies ran while one was open for 2% of the time, Pallas kernels for 23%

profile of v1, /device:TPU:96, one launch (start us, length us, event | category | flops | bytes accessed | tf_op | source)
XLA Modules:
  0.0 251.3 jit_solution(9908588325675401874)
XLA Ops:
  0.0 0.7 copy-done.13
  0.7 2.1 copy-done.15
  2.8 0.7 copy-done.17
  3.5 7.2 %pack_values.1 = bf16[16,4,2,96,128]{4,3,2,1,0:T(8,128)(2,1)S(1)} custom-call(s32[5]{0:T(128)S(1)} %copy-done.13, s32[12,128]{1,0:T(8,128)S(1)} %bitcast.5, bf16[3072,640]{1,0:T(8,128)(2,1)S(1)} %copy-done.15), custom_call_target="tpu_custom_call" | custom-call | flops 4831838208 | bytes 7864320 | tf_op jit(solution)/shard_map/pack_values/pallas_call | solution.py:123
  10.6 1.7 copy-done.12
  12.3 7.2 %all-to-all-start = ((bf16[16,4,2,96,128]{4,3,2,1,0:T(8,128)(2,1)}), bf16[16,4,2,96,128]{4,3,2,1,0:T(8,128)(2,1)S(1)}, u32[]{:S(2)}, u32[]{:S(2)}) async-start(bf16[16,4,2,96,128]{4,3,2,1,0:T(8,128)(2,1)} %copy-done.12), calls=%async_computation | async-start | bytes 6291456 | tf_op jit(solution)/shard_map/all_to_all | solution.py:390
  19.6 2.1 copy-done.6
  21.7 2.1 copy-done.9
  23.8 1.7 square_sums.1
  25.5 22.3 %psum.7.sums_ref = f32[2,2,12,128]{3,2,1,0:T(8,128)S(1)} all-reduce(f32[2,2,12,128]{3,2,1,0:T(8,128)S(1)} %square_sums.1), channel_id=1, replica_groups=mesh['seq'=16,'head'=8] {'head'}, use_global_device_ids=true, to_apply=%region_0.1 | all-reduce | flops 6144 | bytes 49152 | tf_op jit(solution)/shard_map/psum | solution.py:417
  47.8 2.1 copy-done.7
  49.9 2.1 copy-done.10
  52.1 15.1 %pack_norms.1 = (bf16[16,3,2,2,96,128]{5,4,3,2,1,0:T(8,128)(2,1)S(1)}, bf16[16,1,2,2,96,128]{5,4,3,2,1,0:T(8,128)(2,1)}) custom-call(s32[5]{0:T(128)S(1)} %copy-done.14, s32[12,128]{1,0:T(8,128)S(1)} %bitcast.6, f32[2,2,12,128]{3,2,1,0:T(8,128)S(1)} %psum.7.sums_ref, f32[2,1,640]{2,1,0:T(1,128)S(1)} %broadcast_in_dim.34.gain_ref, ...), custom_call_target="tpu_custom_call" | custom-call | flops 9663676416 | bytes 15728640 | tf_op jit(solution)/shard_map/pack_norms/pallas_call | solution.py:194
  67.1 2.2 copy-done.5
  69.3 1.7 copy-done
  71.0 6.8 %all-to-all-start.1 = ((bf16[16,3,2,2,96,128]{5,4,3,2,1,0:T(8,128)(2,1)}), bf16[16,3,2,2,96,128]{5,4,3,2,1,0:T(8,128)(2,1)}, u32[]{:S(2)}, u32[]{:S(2)}) async-start(bf16[16,3,2,2,96,128]{5,4,3,2,1,0:T(8,128)(2,1)} %copy-done.5), calls=%async_computation.1 | async-start | bytes 9437184 | tf_op jit(solution)/shard_map/all_to_all | solution.py:390
  78.1 2.1 copy-done.8
  80.2 2.1 copy-done.11
  82.3 2.1 copy-done.16
  84.5 21.8 %frame_attention.1.spatial_ref = bf16[3072,128]{1,0:T(8,128)(2,1)S(1)} custom-call(s32[5]{0:T(128)S(1)} %copy-done.14, f32[5,12,1536]{2,1,0:T(8,128)S(1)} %reshape.38.bias_ref, f32[2,2,12,128]{3,2,1,0:T(8,128)S(1)} %psum.7.sums_ref, f32[2,1,640]{2,1,0:T(1,128)S(1)} %broadcast_in_dim.34.gain_ref, bf16[3072,640]{1,0:T(8,128)(2,1)S(1)} %copy-done.8, ...), custom_call_target="tpu_custom_call" | custom-call | flops 4831838208 | bytes 3145728 | tf_op jit(solution)/shard_map/frame_attention/pallas_call | solution.py:309
  106.2 35.8 %all-to-all-done.1.q_ref.k_ref = bf16[16,3,2,2,96,128]{5,4,3,2,1,0:T(8,128)(2,1)} async-done(((bf16[16,3,2,2,96,128]{5,4,3,2,1,0:T(8,128)(2,1)}), bf16[16,3,2,2,96,128]{5,4,3,2,1,0:T(8,128)(2,1)}, u32[]{:S(2)}, u32[]{:S(2)}) %all-to-all-start.1) | async-done | bytes 4718624 | tf_op jit(solution)/shard_map/all_to_all | solution.py:390
  142.1 15.5 %all-to-all-start.2 = ((bf16[16,1,2,2,96,128]{5,4,3,2,1,0:T(8,128)(2,1)}), bf16[16,1,2,2,96,128]{5,4,3,2,1,0:T(8,128)(2,1)S(1)}, u32[]{:S(2)}, u32[]{:S(2)}) async-start(bf16[16,1,2,2,96,128]{5,4,3,2,1,0:T(8,128)(2,1)} %get-tuple-element.22), calls=%async_computation.2 | async-start | bytes 3145728 | tf_op jit(solution)/shard_map/all_to_all | solution.py:390
  157.8 1.7 tile.11
  159.5 2.7 %tile.12.bias_ref = f32[5,32,1024]{2,1,0:T(8,128)S(1)} reshape(f32[5,32,32,32]{3,2,1,0:T(8,128)} %tile.11) | data formatting | bytes 1310720 | tf_op jit(solution)/shard_map/tile | solution.py:409
  162.2 1.9 copy-done.1
  164.1 20.4 %window_attention.2.rest_0_ = bf16[16,4,2,96,128]{4,3,2,1,0:T(8,128)(2,1)S(1)} custom-call(s32[5]{0:T(128)S(1)} %copy-done.14, f32[5,32,1024]{2,1,0:T(8,128)S(1)} %tile.12.bias_ref, bf16[16,3,2,2,96,128]{5,4,3,2,1,0:T(8,128)(2,1)} %all-to-all-done.1.q_ref.k_ref, bf16[16,3,2,2,96,128]{5,4,3,2,1,0:T(8,128)(2,1)} %all-to-all-done.1.q_ref.k_ref, ...), custom_call_target="tpu_custom_call" | custom-call | flops 9663676416 | bytes 9437184 | tf_op jit(solution)/shard_map/window_attention/pallas_call | solution.py:268
  184.5 1.6 copy-done.3
  186.2 1.9 copy-done.2
  188.1 1.9 copy-done.4
  190.0 6.9 %window_attention.3 = bf16[16,4,2,96,128]{4,3,2,1,0:T(8,128)(2,1)S(1)} custom-call(s32[5]{0:T(128)S(1)} %copy-done.14, f32[5,32,1024]{2,1,0:T(8,128)S(1)} %tile.12.bias_ref, bf16[16,1,2,2,96,128]{5,4,3,2,1,0:T(8,128)(2,1)S(1)} %all-to-all-done.2.q_ref.k_ref, ...), custom_call_target="tpu_custom_call", output_to_operand_aliasing={{}: (5, {})} | custom-call | flops 3221225472 | bytes 3145728 | tf_op jit(solution)/shard_map/window_attention/pallas_call | solution.py:268
  196.9 46.2 %all_to_all.20.moved_ref = bf16[16,4,2,96,128]{4,3,2,1,0:T(8,128)(2,1)S(1)} all-to-all(bf16[16,4,2,96,128]{4,3,2,1,0:T(8,128)(2,1)S(1)} %window_attention.3), channel_id=1, replica_groups=mesh['seq'=16,'head'=8] {'seq'}, dimensions={0} | all-to-all | bytes 6291456 | tf_op jit(solution)/shard_map/all_to_all | solution.py:390
  243.1 8.2 %unpack.1 = bf16[3072,640]{1,0:T(8,128)(2,1)} custom-call(s32[5]{0:T(128)S(1)} %copy-done.14, s32[12,128]{1,0:T(8,128)S(1)} %bitcast.7, bf16[3072,128]{1,0:T(8,128)(2,1)S(1)} %frame_attention.1.spatial_ref, bf16[16,4,2,96,128]{4,3,2,1,0:T(8,128)(2,1)S(1)} %all_to_all.20.moved_ref), custom_call_target="tpu_custom_call" | custom-call | flops 4831838208 | bytes 7864320 | tf_op jit(solution)/shard_map/unpack/pallas_call | solution.py:362
  (45 shorter events, 0.6 us)
Async XLA Ops:
  0.0 0.7 copy-start.13
  0.7 2.1 copy-start.15
  2.8 0.7 copy-start.17
  10.6 1.7 copy-start.12
  12.3 7.2 %copy-start.21 = (f32[640]{0:T(1024)S(1)}, f32[640]{0:T(1024)}, u32[]{:S(2)}) copy-start(f32[640]{0:T(1024)} %param.13) | copy-start | bytes 7684
  12.3 7.2 %copy-start.22 = (f32[640]{0:T(1024)S(1)}, f32[640]{0:T(1024)}, u32[]{:S(2)}) copy-start(f32[640]{0:T(1024)} %param.12) | copy-start | bytes 7684
  12.3 57.0 %all-to-all-start = ((bf16[16,4,2,96,128]{4,3,2,1,0:T(8,128)(2,1)}), bf16[16,4,2,96,128]{4,3,2,1,0:T(8,128)(2,1)S(1)}, u32[]{:S(2)}, u32[]{:S(2)}) async-start(bf16[16,4,2,96,128]{4,3,2,1,0:T(8,128)(2,1)} %copy-done.12), calls=%async_computation | async-start | bytes 6291456 | tf_op jit(solution)/shard_map/all_to_all | solution.py:390
  19.5 2.1 copy-start.6
  21.7 2.1 copy-start.9
  23.8 24.0 %copy-start.14 = (s32[5]{0:T(128)S(1)}, s32[5]{0:T(128)}, u32[]{:S(2)}) copy-start(s32[5]{0:T(128)} %class_ref.11) | copy-start | bytes 64
  23.8 24.0 %copy-start.18 = (s32[1536]{0:T(1024)S(1)}, s32[1536]{0:T(1024)}, u32[]{:S(2)}) copy-start(s32[1536]{0:T(1024)} %param.17) | copy-start | bytes 18436
  47.8 2.1 copy-start.7
  49.9 2.1 copy-start.10
  67.1 2.2 copy-start.5
  69.3 1.7 copy-start
  69.3 8.5 %copy-start.19 = (s32[5,12,12]{2,1,0:T(8,128)S(1)}, s32[5,12,12]{2,1,0:T(8,128)}, u32[]{:S(2)}) copy-start(s32[5,12,12]{2,1,0:T(8,128)} %param.15) | copy-start | bytes 8644
  71.0 71.1 %all-to-all-start.1 = ((bf16[16,3,2,2,96,128]{5,4,3,2,1,0:T(8,128)(2,1)}), bf16[16,3,2,2,96,128]{5,4,3,2,1,0:T(8,128)(2,1)}, u32[]{:S(2)}, u32[]{:S(2)}) async-start(bf16[16,3,2,2,96,128]{5,4,3,2,1,0:T(8,128)(2,1)} %copy-done.5), calls=%async_computation.1 | async-start | bytes 9437184 | tf_op jit(solution)/shard_map/all_to_all | solution.py:390
  78.1 2.1 copy-start.8
  80.2 2.1 copy-start.11
  82.3 2.1 copy-start.16
  106.2 51.4 %copy-start.20 = (s32[5,8,8]{2,1,0:T(8,128)S(1)}, s32[5,8,8]{2,1,0:T(8,128)}, u32[]{:S(2)}) copy-start(s32[5,8,8]{2,1,0:T(8,128)} %param.16) | copy-start | bytes 3844
  142.1 44.1 %all-to-all-start.2 = ((bf16[16,1,2,2,96,128]{5,4,3,2,1,0:T(8,128)(2,1)}), bf16[16,1,2,2,96,128]{5,4,3,2,1,0:T(8,128)(2,1)S(1)}, u32[]{:S(2)}, u32[]{:S(2)}) async-start(bf16[16,1,2,2,96,128]{5,4,3,2,1,0:T(8,128)(2,1)} %get-tuple-element.22), calls=%async_computation.2 | async-start | bytes 3145728 | tf_op jit(solution)/shard_map/all_to_all | solution.py:390
  162.2 1.9 copy-start.1
  184.5 1.6 copy-start.3
  186.2 1.9 copy-start.2
  188.1 1.9 copy-start.4

commit v2 on v1

v2 whole, which is shorter than its diff:
```python
import functools

import jax
import jax.numpy as jnp
from jax import lax
from jax.experimental import pallas as pl
from jax.experimental.pallas import tpu as pltpu
from jax.sharding import PartitionSpec as P

HEADS = 40
HEAD_DIM = 128
LOCATIONS = 1536
BLOCK = 128
WINDOW_SPAN = 32
GROUP = 5
TEMPORAL = 4
FEATURES = HEADS * HEAD_DIM
EPSILON = 1e-06
MASKED = -(2.0**100)
EXP2_SCALE = 1.4426950408889634 * HEAD_DIM ** (-0.5)
LANE_BLOCKS = LOCATIONS // 128
PAIR = 2
VMEM_LIMIT = 60 * 2**20

F32 = jnp.float32
BF16 = jnp.bfloat16


def params(vmem=VMEM_LIMIT):
    return pltpu.CompilerParams(vmem_limit_bytes=vmem)


def cost(flops, nbytes, exps=0):
    return pl.CostEstimate(flops=int(flops), bytes_accessed=int(nbytes), transcendentals=int(exps))


def spatial_head(class_ref):
    found = jnp.int32(0)
    for i in range(1, GROUP):
        found = found + i * (1 - class_ref[i])
    return found


def temporal_head(class_ref, j):
    return j + (j >= spatial_head(class_ref)).astype(jnp.int32)


def column(row):
    return jnp.broadcast_to(row, (128, 128)).T


def sums_kernel(q_ref, k_ref, out_ref):
    for a, ref in enumerate((q_ref, k_ref)):
        for i in range(q_ref.shape[0] // 128):
            part = jnp.zeros((128, 128), F32)
            for j in range(GROUP):
                x = ref[128 * i : 128 * i + 128, 128 * j : 128 * j + 128].astype(F32)
                part = part + x * x
            out_ref[a, 0, 0, i, :] = jnp.sum(part.T, axis=0)


def square_sums(query_proj, key_proj):
    tokens, features = query_proj.shape
    frames = tokens // LOCATIONS
    parts = 3
    in_spec = pl.BlockSpec((LOCATIONS // parts, features), lambda f, i: (f * parts + i, 0))
    return pl.pallas_call(
        sums_kernel,
        grid=(frames, parts),
        in_specs=[in_spec, in_spec],
        out_specs=pl.BlockSpec(
            (2, 1, 1, LANE_BLOCKS // parts, 128), lambda f, i: (0, f, i, 0, 0)
        ),
        out_shape=jax.ShapeDtypeStruct((2, frames, parts, LANE_BLOCKS // parts, 128), F32),
        compiler_params=params(),
        cost_estimate=cost(4 * tokens * features, 4 * tokens * features),
        name="square_sums",
    )(query_proj, key_proj)


def build_picked(order_ref, picked_ref):
    lanes = lax.broadcasted_iota(jnp.int32, (128, 128), 1).astype(F32)
    for i in range(LANE_BLOCKS):
        wanted = column(order_ref[i : i + 1, :].astype(F32))
        for j in range(LANE_BLOCKS):
            hit = wanted == lanes + float(128 * j)
            picked_ref[128 * i : 128 * i + 128, 128 * j : 128 * j + 128] = jnp.where(
                hit, 1.0, 0.0
            ).astype(BF16)


def pick_rows(picked_ref, heads_ref, store):
    rows = 384
    for c in range(LOCATIONS // rows):
        y = jnp.dot(
            picked_ref[rows * c : rows * c + rows, :],
            heads_ref[...],
            preferred_element_type=F32,
        ).astype(BF16)
        store(c, rows, y)


def pack_value_kernel(class_ref, order_ref, x_ref, out_ref, picked_ref, heads_ref):
    @pl.when(pl.program_id(0) == 0)
    def _():
        build_picked(order_ref, picked_ref)

    for j in range(TEMPORAL):
        h = temporal_head(class_ref, j)
        heads_ref[:, 128 * j : 128 * j + 128] = x_ref[
            :, pl.ds(pl.multiple_of(h * 128, 128), 128)
        ]

    def store(c, rows, y):
        slots = rows // 96
        for j in range(TEMPORAL):
            out_ref[slots * c : slots * c + slots, j, 0] = y[
                :, 128 * j : 128 * j + 128
            ].reshape(slots, 96, 128)

    pick_rows(picked_ref, heads_ref, store)


def pack_values(value_proj, head_class, order):
    tokens, features = value_proj.shape
    frames = tokens // LOCATIONS
    return pl.pallas_call(
        pack_value_kernel,
        grid_spec=pltpu.PrefetchScalarGridSpec(
            num_scalar_prefetch=1,
            grid=(frames,),
            in_specs=[
                pl.BlockSpec((LANE_BLOCKS, 128), lambda f, c: (0, 0)),
                pl.BlockSpec((LOCATIONS, features), lambda f, c: (f, 0)),
            ],
            out_specs=pl.BlockSpec((16, TEMPORAL, 1, 96, 128), lambda f, c: (0, 0, f, 0, 0)),
            scratch_shapes=[
                pltpu.VMEM((LOCATIONS, LOCATIONS), BF16),
                pltpu.VMEM((LOCATIONS, TEMPORAL * 128), BF16),
            ],
        ),
        out_shape=jax.ShapeDtypeStruct((16, TEMPORAL, frames, 96, 128), BF16),
        compiler_params=params(),
        cost_estimate=cost(2 * tokens * LOCATIONS * 512, 4 * tokens * features),
        name="pack_values",
    )(head_class, order, value_proj)


def factor_of(sums):
    return lax.rsqrt(sums * (1.0 / FEATURES) + EPSILON)


def pack_norm_kernel(
    class_ref, turn_ref, order_ref, sums_ref, gain0_ref, gain1_ref, q0_ref, q1_ref, k0_ref, k1_ref, *rest
):
    before_ref, (out_ref, picked_ref, heads_ref) = rest[:-3], rest[-3:]
    mine = turn_ref[0] != 0
    array = pl.program_id(0)

    @pl.when(mine & (array == 0) & (pl.program_id(1) == 0))
    def _():
        build_picked(order_ref, picked_ref)

    def load(refs):
        factor = factor_of(sums_ref[0, 0])
        for i in range(LANE_BLOCKS):
            scale = column(factor[i : i + 1, :])
            for j, (x_ref, gain_ref) in enumerate(zip(refs, (gain0_ref, gain1_ref))):
                x = x_ref[128 * i : 128 * i + 128, :].astype(F32)
                heads_ref[128 * i : 128 * i + 128, 128 * j : 128 * j + 128] = (
                    x * scale * gain_ref[0]
                ).astype(BF16)

    @pl.when(mine & (array == 0))
    def _():
        load((q0_ref, q1_ref))

    @pl.when(mine & (array == 1))
    def _():
        load((k0_ref, k1_ref))

    @pl.when(mine)
    def _():
        def store(c, rows, y):
            slots = rows // 96
            for j in range(PAIR):
                out_ref[slots * c : slots * c + slots, j, 0, 0] = y[
                    :, 128 * j : 128 * j + 128
                ].reshape(slots, 96, 128)

        pick_rows(picked_ref, heads_ref, store)

    if before_ref:

        @pl.when(jnp.logical_not(mine))
        def _():
            out_ref[...] = before_ref[0][...]


def pack_norms(query_proj, key_proj, sums, gains, head_class, order, first, turn, before=None):
    tokens, features = query_proj.shape
    frames = tokens // LOCATIONS

    def head_spec(array, j):
        def index(a, f, c, t):
            frame = f * (1 - a) + a * (frames - 1) if array == 0 else f * a
            return (frame * t[0], temporal_head(c, first + j))

        return pl.BlockSpec((LOCATIONS, 128), index)

    def gain_spec(j):
        return pl.BlockSpec((1, 1, 128), lambda a, f, c, t: (a, 0, temporal_head(c, first + j)))

    out_spec = pl.BlockSpec(
        (16, PAIR, 1, 1, 96, 128), lambda a, f, c, t: (0, 0, a * t[0], f * t[0], 0, 0)
    )
    in_specs = [
        pl.BlockSpec((LANE_BLOCKS, 128), lambda a, f, c, t: (0, 0)),
        pl.BlockSpec((1, 1, LANE_BLOCKS, 128), lambda a, f, c, t: (a, f, 0, 0)),
        gain_spec(0),
        gain_spec(1),
        head_spec(0, 0),
        head_spec(0, 1),
        head_spec(1, 0),
        head_spec(1, 1),
    ]
    operands = [
        head_class, turn, order, sums, gains, gains, query_proj, query_proj, key_proj, key_proj
    ]
    aliases = {}
    if before is not None:
        in_specs.append(
            pl.BlockSpec((16, PAIR, 1, 1, 96, 128), lambda a, f, c, t: (0, 0, 0, 0, 0, 0))
        )
        aliases = {len(operands): 0}
        operands.append(before)
    return pl.pallas_call(
        pack_norm_kernel,
        grid_spec=pltpu.PrefetchScalarGridSpec(
            num_scalar_prefetch=2,
            grid=(2, frames),
            in_specs=in_specs,
            out_specs=out_spec,
            scratch_shapes=[
                pltpu.VMEM((LOCATIONS, LOCATIONS), BF16),
                pltpu.VMEM((LOCATIONS, PAIR * 128), BF16),
            ],
        ),
        out_shape=jax.ShapeDtypeStruct((16, PAIR, 2, frames, 96, 128), BF16),
        input_output_aliases=aliases,
        compiler_params=params(),
        cost_estimate=cost(4 * tokens * LOCATIONS * 256, 8 * tokens * 256),
        name="pack_norms",
    )(*operands)


def softmax_rows(queries, key_rows, values, bias=None):
    s = lax.dot_general(
        queries, key_rows, (((1,), (1,)), ((), ())), preferred_element_type=F32
    )
    if bias is not None:
        s = s + bias
    top = jnp.max(s, axis=1, keepdims=True)
    w = jnp.exp2((s - top) * EXP2_SCALE)
    total = jnp.sum(w, axis=1, keepdims=True)
    mixture = jnp.dot(w.astype(BF16), values, preferred_element_type=F32)
    return (mixture / total).astype(BF16)


def window_kernel(class_ref, bias_ref, q_ref, k_ref, v_ref, out_ref, wide_q_ref, wide_k_ref):
    tokens = 16 * 2 * WINDOW_SPAN

    @pl.when((pl.program_id(0) == 0) & (pl.program_id(1) == 0))
    def _():
        place = lax.broadcasted_iota(jnp.int32, (tokens, 128), 0) % WINDOW_SPAN
        lane = lax.broadcasted_iota(jnp.int32, (tokens, 128), 1)
        wide_q_ref[:, 128:] = jnp.where(place // 4 == lane, 1.0, 0.0).astype(BF16)

    @pl.when(pl.program_id(1) == 0)
    def _():
        repeated = jnp.broadcast_to(bias_ref[...], (32, WINDOW_SPAN, 128))
        wide_k_ref[:, 128:] = repeated.reshape(tokens, 128).astype(BF16)

    wide_q_ref[:, :128] = q_ref[...].reshape(tokens, 128)
    wide_k_ref[:, :128] = k_ref[...].reshape(tokens, 128)
    v = v_ref[...].reshape(tokens, 128)
    rows = 256
    for c in range(tokens // rows):
        o = softmax_rows(wide_q_ref[rows * c : rows * c + rows, :], wide_k_ref[...], v)
        slots = rows // (2 * WINDOW_SPAN)
        out_ref[slots * c : slots * c + slots, 0] = o.reshape(slots, 2, WINDOW_SPAN, 128)


def window_attention(moved, values, bias, head_class, first):
    count = moved.shape[1]
    windows = 96 // WINDOW_SPAN
    block = (16, 1, 2, WINDOW_SPAN, 128)
    qk_block = (16, 1, 1, 2, WINDOW_SPAN, 128)
    return pl.pallas_call(
        window_kernel,
        grid_spec=pltpu.PrefetchScalarGridSpec(
            num_scalar_prefetch=1,
            grid=(count, windows),
            in_specs=[
                pl.BlockSpec(
                    (1, WINDOW_SPAN, 128), lambda h, w, c: (temporal_head(c, h + first), 0, 0)
                ),
                pl.BlockSpec(qk_block, lambda h, w, c: (0, h, 0, 0, w, 0)),
                pl.BlockSpec(qk_block, lambda h, w, c: (0, h, 1, 0, w, 0)),
                pl.BlockSpec(block, lambda h, w, c: (0, h + first, 0, w, 0)),
            ],
            out_specs=pl.BlockSpec(block, lambda h, w, c: (0, h, 0, w, 0)),
            scratch_shapes=[
                pltpu.VMEM((16 * 2 * WINDOW_SPAN, 256), BF16),
                pltpu.VMEM((16 * 2 * WINDOW_SPAN, 256), BF16),
            ],
        ),
        out_shape=jax.ShapeDtypeStruct((16, count, 2, 96, 128), BF16),
        compiler_params=params(),
        cost_estimate=cost(
            8 * count * windows * 1024 * 1024 * 128, 8 * count * windows * 1024 * 128, count * windows * 1024 * 1024
        ),
        name="window_attention",
    )(head_class, bias, moved, moved, values)


def frame_kernel(class_ref, turn_ref, bias_ref, sums_ref, gain_ref, q_ref, k_ref, v_ref, *rest):
    before_ref, (out_ref, qn_ref, kn_ref) = rest[:-3], rest[-3:]

    @pl.when(turn_ref[0] != 0)
    def _():
        for a, (x_ref, n_ref) in enumerate(((q_ref, qn_ref), (k_ref, kn_ref))):
            factor = factor_of(sums_ref[a, 0])
            for i in range(LANE_BLOCKS):
                x = x_ref[128 * i : 128 * i + 128, :].astype(F32)
                n_ref[128 * i : 128 * i + 128, :] = (
                    x * column(factor[i : i + 1, :]) * gain_ref[a]
                ).astype(BF16)

        def body(i, carry):
            rows = pl.ds(pl.multiple_of(i * 128, 128), 128)
            out_ref[rows, :] = softmax_rows(
                qn_ref[rows, :], kn_ref[...], v_ref[...], bias_ref[0, pl.ds(i, 1), :]
            )
            return carry

        lax.fori_loop(0, LANE_BLOCKS, body, 0)

    if before_ref:

        @pl.when(turn_ref[0] == 0)
        def _():
            out_ref[...] = before_ref[0][...]


def frame_attention(query_proj, key_proj, value_proj, sums, gains, bias, head_class, turn, before=None):
    tokens = query_proj.shape[0]
    frames = tokens // LOCATIONS
    column_spec = pl.BlockSpec((LOCATIONS, 128), lambda f, c, t: (f * t[0], spatial_head(c)))
    out_spec = pl.BlockSpec((LOCATIONS, 128), lambda f, c, t: (f * t[0], 0))
    in_specs = [
        pl.BlockSpec((1, LANE_BLOCKS, LOCATIONS), lambda f, c, t: (spatial_head(c), 0, 0)),
        pl.BlockSpec((2, 1, LANE_BLOCKS, 128), lambda f, c, t: (0, f, 0, 0)),
        pl.BlockSpec((2, 1, 128), lambda f, c, t: (0, 0, spatial_head(c))),
        column_spec,
        column_spec,
        column_spec,
    ]
    operands = [head_class, turn, bias, sums, gains, query_proj, key_proj, value_proj]
    aliases = {}
    if before is not None:
        in_specs.append(pl.BlockSpec((LOCATIONS, 128), lambda f, c, t: (0, 0)))
        aliases = {len(operands): 0}
        operands.append(before)
    return pl.pallas_call(
        frame_kernel,
        grid_spec=pltpu.PrefetchScalarGridSpec(
            num_scalar_prefetch=2,
            grid=(frames,),
            in_specs=in_specs,
            out_specs=out_spec,
            scratch_shapes=[
                pltpu.VMEM((LOCATIONS, 128), BF16),
                pltpu.VMEM((LOCATIONS, 128), BF16),
            ],
        ),
        out_shape=jax.ShapeDtypeStruct((tokens, 128), BF16),
        input_output_aliases=aliases,
        compiler_params=params(),
        cost_estimate=cost(
            4 * tokens * LOCATIONS * 256, 8 * tokens * 128, tokens * LOCATIONS
        ),
        name="frame_attention",
    )(*operands)


def place_rows(order_ref, moved_ref, heads_ref, first, rows):
    count = moved_ref.shape[1]
    for j in range(count):
        heads_ref[:, 128 * j : 128 * j + 128] = moved_ref[:, j, 0].reshape(LOCATIONS, 128)
    places = lax.broadcasted_iota(jnp.int32, (rows, 128), 0) + first
    parts = []
    for i in range(LANE_BLOCKS):
        hit = order_ref[i : i + 1, :] == places
        parts.append(jnp.where(hit, 1.0, 0.0).astype(BF16))
    return jnp.dot(
        jnp.concatenate(parts, axis=1), heads_ref[...], preferred_element_type=F32
    ).astype(BF16)


def unpack_kernel(order_ref, moved_ref, out_ref, heads_ref):
    rows = out_ref.shape[0]
    out_ref[...] = place_rows(order_ref, moved_ref, heads_ref, pl.program_id(1) * rows, rows)


def join_kernel(class_ref, order_ref, moved_ref, early_ref, spatial_ref, out_ref, heads_ref):
    rows = out_ref.shape[0]
    y = place_rows(order_ref, moved_ref, heads_ref, pl.program_id(1) * rows, rows)
    early = early_ref.shape[1] // 128
    for j in range(TEMPORAL):
        h = pl.multiple_of(temporal_head(class_ref, j) * 128, 128)
        if j < early:
            out_ref[:, pl.ds(h, 128)] = early_ref[:, 128 * j : 128 * j + 128]
        else:
            i = j - early
            out_ref[:, pl.ds(h, 128)] = y[:, 128 * i : 128 * i + 128]
    h = pl.multiple_of(spatial_head(class_ref) * 128, 128)
    out_ref[:, pl.ds(h, 128)] = spatial_ref[...]


UNPACK_ROWS = 768


def unpack(returned, order):
    count, frames = returned.shape[1:3]
    tokens = frames * LOCATIONS
    rows = UNPACK_ROWS
    steps = LOCATIONS // rows
    return pl.pallas_call(
        unpack_kernel,
        grid=(frames, steps),
        in_specs=[
            pl.BlockSpec((LANE_BLOCKS, 128), lambda f, i: (0, 0)),
            pl.BlockSpec((16, count, 1, 96, 128), lambda f, i: (0, 0, f, 0, 0)),
        ],
        out_specs=pl.BlockSpec((rows, count * 128), lambda f, i: (f * steps + i, 0)),
        scratch_shapes=[pltpu.VMEM((LOCATIONS, count * 128), BF16)],
        out_shape=jax.ShapeDtypeStruct((tokens, count * 128), BF16),
        compiler_params=params(),
        cost_estimate=cost(2 * tokens * LOCATIONS * 128 * count, 4 * tokens * 128 * count),
        name="unpack",
    )(order, returned)


def join(returned, early, spatial_out, head_class, order):
    count, frames = returned.shape[1:3]
    tokens = frames * LOCATIONS
    rows = UNPACK_ROWS
    steps = LOCATIONS // rows
    return pl.pallas_call(
        join_kernel,
        grid_spec=pltpu.PrefetchScalarGridSpec(
            num_scalar_prefetch=1,
            grid=(frames, steps),
            in_specs=[
                pl.BlockSpec((LANE_BLOCKS, 128), lambda f, i, c: (0, 0)),
                pl.BlockSpec((16, count, 1, 96, 128), lambda f, i, c: (0, 0, f, 0, 0)),
                pl.BlockSpec((rows, early.shape[1]), lambda f, i, c: (f * steps + i, 0)),
                pl.BlockSpec((rows, 128), lambda f, i, c: (f * steps + i, 0)),
            ],
            out_specs=pl.BlockSpec((rows, GROUP * 128), lambda f, i, c: (f * steps + i, 0)),
            scratch_shapes=[pltpu.VMEM((LOCATIONS, count * 128), BF16)],
        ),
        out_shape=jax.ShapeDtypeStruct((tokens, GROUP * 128), BF16),
        compiler_params=params(),
        cost_estimate=cost(2 * tokens * LOCATIONS * 128 * count, 4 * tokens * 640),
        name="join",
    )(head_class, order, returned, early, spatial_out)


def spread_mask(mask, repeat):
    blocks = mask.shape[-1]
    same = jnp.arange(blocks)[:, None] == jnp.arange(blocks)[None, :]
    bias = jnp.where((mask != 0) | same, 0.0, MASKED).astype(F32)
    return jnp.repeat(bias, repeat, axis=2)


def exchange(tensor):
    return lax.all_to_all(tensor, "seq", split_axis=0, concat_axis=0, tiled=True)


def sum_over_heads(sums):
    size = lax.axis_size("head")
    step = 1
    while step < size:
        pairs = [(i, i ^ step) for i in range(size)]
        sums = sums + lax.ppermute(sums, "head", pairs)
        step *= 2
    return sums


def shards(
    query_proj,
    key_proj,
    value_proj,
    query_gain,
    key_gain,
    head_class,
    spatial_mask,
    temporal_mask,
    location_order,
):
    order = location_order.reshape(LANE_BLOCKS, 128)
    gains = jnp.stack([query_gain, key_gain])[:, None, :]
    window_bias = jnp.pad(
        jnp.repeat(jnp.swapaxes(spread_mask(temporal_mask, 1), 1, 2), 4, axis=1),
        ((0, 0), (0, 0), (0, 120)),
    )
    frame_bias = spread_mask(spatial_mask, 128)
    late = (lax.axis_index("head") % 2).astype(jnp.int32).reshape(1)
    always = jnp.ones((1,), jnp.int32)

    def norms(first, turn, before=None):
        return pack_norms(
            query_proj, key_proj, sums, gains, head_class, order, first, turn, before
        )

    def within_frames(turn, before=None):
        return frame_attention(
            query_proj, key_proj, value_proj, sums, gains, frame_bias, head_class, turn, before
        )

    packed_values = pack_values(value_proj, head_class, order)
    values = exchange(packed_values)
    query_proj, key_proj, packed_values = lax.optimization_barrier(
        (query_proj, key_proj, packed_values)
    )
    sums = sum_over_heads(square_sums(query_proj, key_proj)).reshape(2, -1, LANE_BLOCKS, 128)
    first = norms(0, always)
    second = norms(PAIR, late)
    spatial_out = within_frames(late)
    values, first, second, spatial_out = lax.optimization_barrier(
        (values, first, second, spatial_out)
    )

    moved = exchange(first)
    second = norms(PAIR, 1 - late, second)
    spatial_out = within_frames(1 - late, spatial_out)
    moved, spatial_out, second = lax.optimization_barrier((moved, spatial_out, second))

    moved_later = exchange(second)
    mixed = window_attention(moved, values, window_bias, head_class, 0)
    mixed, moved_later = lax.optimization_barrier((mixed, moved_later))

    returned = exchange(mixed)
    mixed = window_attention(moved_later, values, window_bias, head_class, PAIR)
    returned, mixed = lax.optimization_barrier((returned, mixed))

    last = exchange(mixed)
    early = unpack(returned, order)
    last, early = lax.optimization_barrier((last, early))
    return join(last, early, spatial_out, head_class, order)


def solution(mesh):
    return jax.shard_map(
        shards,
        mesh=mesh,
        in_specs=(
            P("seq", "head"),
            P("seq", "head"),
            P("seq", "head"),
            P("head"),
            P("head"),
            P("head"),
            P("head", None, None),
            P("head", None, None),
            P(),
        ),
        out_specs=P("seq", "head"),
        check_vma=False,
    )
```

time: 252 us -> 206 us (0.82)
  the two profiles are of different devices: /device:TPU:96 before, /device:TPU:1 now
where the time goes in v2:
time: 206 us; the launch traced here: 205 us
  Pallas kernels  110 us (53%)
  starting transfers between devices  44.3 us (22%)
  waiting for transfers between devices  41.9 us (20%)
  local copies, waits for them, and re-layouts  7.6 us (4%)
    all_to_all x5, waiting for transfers between devices, exchange(): lax.all_to_all(tensor, 'seq', split_axis=0, concat_axis=0, tiled=True)  39.4 us
    all_to_all x5, starting transfers between devices, exchange(): lax.all_to_all(tensor, 'seq', split_axis=0, concat_axis=0, tiled=True)  38.1 us
    pallas_call x2, Pallas kernels, window_attention(): pl.pallas_call(window_kernel, grid_spec=pltpu.PrefetchScalarGridSpec(num_...  31.7 us
    pallas_call x3, Pallas kernels, pack_norms(): pl.pallas_call(pack_norm_kernel, grid_spec=pltpu.PrefetchScalarGridSpec(n...  27 us
    pallas_call x2, Pallas kernels, frame_attention(): pl.pallas_call(frame_kernel, grid_spec=pltpu.PrefetchScalarGridSpec(num_s...  22 us
    pallas_call x1, Pallas kernels, pack_values(): pl.pallas_call(pack_value_kernel, grid_spec=pltpu.PrefetchScalarGridSpec(...  9.84 us
    pallas_call x1, Pallas kernels, join(): pl.pallas_call(join_kernel, grid_spec=pltpu.PrefetchScalarGridSpec(num_sc...  7.26 us
    pallas_call x1, Pallas kernels, square_sums(): pl.pallas_call(sums_kernel, grid=(frames, parts), in_specs=[in_spec, in_s...  6.24 us
  transfers between devices with their start and end apart: 8, of which 5 were waited for; matrix products, arithmetic and copies ran while one was open for 3% of the time, Pallas kernels for 45%

profile of v2, /device:TPU:1, one launch (start us, length us, event | category | flops | bytes accessed | tf_op | source)
XLA Modules:
  0.0 204.6 jit_solution(488313229344547806)
XLA Ops:
  0.0 9.8 %pack_values.1 = bf16[16,4,2,96,128]{4,3,2,1,0:T(8,128)(2,1)} custom-call(s32[5]{0:T(128)} %class_ref.17, s32[12,128]{1,0:T(8,128)} %bitcast.8, bf16[3072,640]{1,0:T(8,128)(2,1)} %v_ref.3), custom_call_target="tpu_custom_call" | custom-call | flops 4831838208 | bytes 7864320 | tf_op jit(solution)/shard_map/pack_values/pallas_call | solution.py:127
  9.8 7.6 %all-to-all-start = ((bf16[16,4,2,96,128]{4,3,2,1,0:T(8,128)(2,1)}), bf16[16,4,2,96,128]{4,3,2,1,0:T(8,128)(2,1)S(1)}, u32[]{:S(2)}, u32[]{:S(2)}) async-start(bf16[16,4,2,96,128]{4,3,2,1,0:T(8,128)(2,1)} %pack_values.1), calls=%async_computation | async-start | bytes 6291456 | tf_op jit(solution)/shard_map/all_to_all | solution.py:489
  17.5 6.2 %square_sums.1 = f32[2,2,3,4,128]{4,3,2,1,0:T(4,128)} custom-call(bf16[3072,640]{1,0:T(8,128)(2,1)} %q1_ref.2, bf16[3072,640]{1,0:T(8,128)(2,1)} %k1_ref.2), custom_call_target="tpu_custom_call" | custom-call | flops 7864320 | bytes 7864320 | tf_op jit(solution)/shard_map/square_sums/pallas_call | solution.py:67
  23.7 1.0 collective-permute-start
  24.7 1.1 collective-permute-done
  25.7 0.7 add.15
  26.5 1.6 collective-permute-start.1
  28.2 1.4 collective-permute-done.1
  29.6 3.5 %collective-permute-start.2 = (f32[2,2,3,4,128]{4,3,2,1,0:T(4,128)S(1)}, f32[2,2,3,4,128]{4,3,2,1,0:T(4,128)S(1)}, u32[]{:S(2)}, u32[]{:S(2)}) collective-permute-start(f32[2,2,3,4,128]{4,3,2,1,0:T(4,128)S(1)} %add.16), channel_id=1, source_target_pairs={{0,4},{1,5},{2,6},{3,7},{4,0},{5,1},{6,2},{7,3},{8,12},{9,13},{10,... | collective-permute-start | bytes 73736 | tf_op jit(solution)/shard_map/ppermute | solution.py:497
  33.2 0.6 broadcast_in_dim.34.gain0_ref.gain1_ref.gain_ref
  33.8 1.0 broadcast_in_dim.37
  34.7 1.9 reshape.43.bias_ref
  36.7 0.6 copy.15.sums_ref
  37.3 11.2 %pack_norms.4.rest_0_ = bf16[16,2,2,2,96,128]{5,4,3,2,1,0:T(8,128)(2,1)} custom-call(s32[5]{0:T(128)} %class_ref.17, s32[1]{0:T(128)} %bitcast.4.turn_ref, s32[12,128]{1,0:T(8,128)} %bitcast.9, f32[2,2,12,128]{3,2,1,0:T(8,128)} %copy.15.sums_ref, f32[2,1,640]{2,1,0:T(1,128)} %broadcast_in_dim.34.gain0_ref.gain1_ref.gain_ref, ...), custom_call_target="tpu_custom_call" | custom-call | flops 4831838208 | bytes 6291456 | tf_op jit(solution)/shard_map/pack_norms/pallas_call | solution.py:237
  48.5 19.0 %frame_attention.2.rest_0_ = bf16[3072,128]{1,0:T(8,128)(2,1)} custom-call(s32[5]{0:T(128)} %class_ref.17, s32[1]{0:T(128)} %bitcast.4.turn_ref, f32[5,12,1536]{2,1,0:T(8,128)} %reshape.43.bias_ref, f32[2,2,12,128]{3,2,1,0:T(8,128)} %copy.15.sums_ref, f32[2,1,640]{2,1,0:T(1,128)} %broadcast_in_dim.34.gain0_ref.gain1_ref.gain_ref, bf16[3072,640]{1,0:T(8,128)(2,1)} %q1_ref.2, ...), custom_call_target="tpu_custom_call" | custom-call | flops 4831838208 | bytes 3145728 | tf_op jit(solution)/shard_map/frame_attention/pallas_call | solution.py:375
  67.5 11.2 %pack_norms.3 = bf16[16,2,2,2,96,128]{5,4,3,2,1,0:T(8,128)(2,1)} custom-call(s32[5]{0:T(128)} %class_ref.17, s32[1]{0:T(128)} %constant.23.clone.1.turn_ref, s32[12,128]{1,0:T(8,128)} %bitcast.10, f32[2,2,12,128]{3,2,1,0:T(8,128)} %copy.15.sums_ref, f32[2,1,640]{2,1,0:T(1,128)} %broadcast_in_dim.34.gain0_ref.gain1_ref.gain_ref, ...), custom_call_target="tpu_custom_call" | custom-call | flops 4831838208 | bytes 6291456 | tf_op jit(solution)/shard_map/pack_norms/pallas_call | solution.py:237
  78.7 1.6 copy-done
  80.3 7.0 %all-to-all-start.1 = ((bf16[16,2,2,2,96,128]{5,4,3,2,1,0:T(8,128)(2,1)}), bf16[16,2,2,2,96,128]{5,4,3,2,1,0:T(8,128)(2,1)}, u32[]{:S(2)}, u32[]{:S(2)}) async-start(bf16[16,2,2,2,96,128]{5,4,3,2,1,0:T(8,128)(2,1)} %pack_norms.3), calls=%async_computation.1 | async-start | bytes 6291456 | tf_op jit(solution)/shard_map/all_to_all | solution.py:489
  87.3 4.6 %pack_norms.5 = bf16[16,2,2,2,96,128]{5,4,3,2,1,0:T(8,128)(2,1)} custom-call(s32[5]{0:T(128)} %class_ref.17, s32[1]{0:T(128)S(6)} %sub.4.turn_ref, s32[12,128]{1,0:T(8,128)} %bitcast.11, f32[2,2,12,128]{3,2,1,0:T(8,128)} %copy.15.sums_ref, f32[2,1,640]{2,1,0:T(1,128)} %broadcast_in_dim.34.gain0_ref.gain1_ref.gain_ref, ...), custom_call_target="tpu_custom_call", output_to_operand_aliasing={{}: (10, {})} | custom-call | flops 4831838208 | bytes 6291456 | tf_op jit(solution)/shard_map/pack_norms/pallas_call | solution.py:237
  91.9 3.1 %frame_attention.3.spatial_ref = bf16[3072,128]{1,0:T(8,128)(2,1)} custom-call(s32[5]{0:T(128)} %class_ref.17, s32[1]{0:T(128)S(6)} %sub.4.turn_ref, f32[5,12,1536]{2,1,0:T(8,128)} %reshape.43.bias_ref, f32[2,2,12,128]{3,2,1,0:T(8,128)} %copy.15.sums_ref, f32[2,1,640]{2,1,0:T(1,128)} %broadcast_in_dim.34.gain0_ref.gain1_ref.gain_ref, ...), custom_call_target="tpu_custom_call", output_to_operand_aliasing={{}: (8, {})} | custom-call | flops 4831838208 | bytes 3145728 | tf_op jit(solution)/shard_map/frame_attention/pallas_call | solution.py:375
  95.0 17.1 %all-to-all-done.1.q_ref.k_ref = bf16[16,2,2,2,96,128]{5,4,3,2,1,0:T(8,128)(2,1)} async-done(((bf16[16,2,2,2,96,128]{5,4,3,2,1,0:T(8,128)(2,1)}), bf16[16,2,2,2,96,128]{5,4,3,2,1,0:T(8,128)(2,1)}, u32[]{:S(2)}, u32[]{:S(2)}) %all-to-all-start.1) | async-done | bytes 3145760 | tf_op jit(solution)/shard_map/all_to_all | solution.py:489
  112.1 8.5 %all-to-all-start.2 = ((bf16[16,2,2,2,96,128]{5,4,3,2,1,0:T(8,128)(2,1)}), bf16[16,2,2,2,96,128]{5,4,3,2,1,0:T(8,128)(2,1)S(1)}, u32[]{:S(2)}, u32[]{:S(2)}) async-start(bf16[16,2,2,2,96,128]{5,4,3,2,1,0:T(8,128)(2,1)} %pack_norms.5), calls=%async_computation.2 | async-start | bytes 6291456 | tf_op jit(solution)/shard_map/all_to_all | solution.py:489
  120.7 0.6 pad.4.bias_ref
  121.4 15.8 %window_attention.2 = bf16[16,2,2,96,128]{4,3,2,1,0:T(8,128)(2,1)} custom-call(s32[5]{0:T(128)} %class_ref.17, f32[5,32,128]{2,1,0:T(8,128)} %pad.4.bias_ref, bf16[16,2,2,2,96,128]{5,4,3,2,1,0:T(8,128)(2,1)} %all-to-all-done.1.q_ref.k_ref, bf16[16,2,2,2,96,128]{5,4,3,2,1,0:T(8,128)(2,1)} %all-to-all-done.1.q_ref.k_ref, bf16[16,4,2,96,128]{4,3,2,1,0:T(8,128)(2,1)} %copy-done), custom_call_target="tpu_custom_call" | custom-call | flops 6442450944 | bytes 6291456 | tf_op jit(solution)/shard_map/window_attention/pallas_call | solution.py:299
  137.2 12.2 %all-to-all-done.2.q_ref.k_ref = bf16[16,2,2,2,96,128]{5,4,3,2,1,0:T(8,128)(2,1)S(1)} async-done(((bf16[16,2,2,2,96,128]{5,4,3,2,1,0:T(8,128)(2,1)}), bf16[16,2,2,2,96,128]{5,4,3,2,1,0:T(8,128)(2,1)S(1)}, u32[]{:S(2)}, u32[]{:S(2)}) %all-to-all-start.2) | async-done | bytes 3145760 | tf_op jit(solution)/shard_map/all_to_all | solution.py:489
  149.4 8.4 %all-to-all-start.3 = ((bf16[16,2,2,96,128]{4,3,2,1,0:T(8,128)(2,1)}), bf16[16,2,2,96,128]{4,3,2,1,0:T(8,128)(2,1)}, u32[]{:S(2)}, u32[]{:S(2)}) async-start(bf16[16,2,2,96,128]{4,3,2,1,0:T(8,128)(2,1)} %window_attention.2), calls=%async_computation.3 | async-start | bytes 3145728 | tf_op jit(solution)/shard_map/all_to_all | solution.py:489
  157.9 15.9 %window_attention.3 = bf16[16,2,2,96,128]{4,3,2,1,0:T(8,128)(2,1)} custom-call(s32[5]{0:T(128)} %class_ref.17, f32[5,32,128]{2,1,0:T(8,128)} %pad.4.bias_ref, bf16[16,2,2,2,96,128]{5,4,3,2,1,0:T(8,128)(2,1)} %copy-done.1, bf16[16,2,2,2,96,128]{5,4,3,2,1,0:T(8,128)(2,1)} %copy-done.1, bf16[16,4,2,96,128]{4,3,2,1,0:T(8,128)(2,1)} %copy-done), custom_call_target="tpu_custom_call" | custom-call | flops 6442450944 | bytes 6291456 | tf_op jit(solution)/shard_map/window_attention/pallas_call | solution.py:299
  173.7 6.6 %all-to-all-start.4 = ((bf16[16,2,2,96,128]{4,3,2,1,0:T(8,128)(2,1)}), bf16[16,2,2,96,128]{4,3,2,1,0:T(8,128)(2,1)S(1)}, u32[]{:S(2)}, u32[]{:S(2)}) async-start(bf16[16,2,2,96,128]{4,3,2,1,0:T(8,128)(2,1)} %window_attention.3), calls=%async_computation.4 | async-start | bytes 3145728 | tf_op jit(solution)/shard_map/all_to_all | solution.py:489
  180.4 5.8 %unpack.1.early_ref = bf16[3072,256]{1,0:T(8,128)(2,1)} custom-call(s32[12,128]{1,0:T(8,128)} %bitcast.12, bf16[16,2,2,96,128]{4,3,2,1,0:T(8,128)(2,1)} %all-to-all-done.3.moved_ref), custom_call_target="tpu_custom_call" | custom-call | flops 2415919104 | bytes 3145728 | tf_op jit(solution)/shard_map/unpack/pallas_call | solution.py:439
  186.1 10.1 %all-to-all-done.4.moved_ref = bf16[16,2,2,96,128]{4,3,2,1,0:T(8,128)(2,1)S(1)} async-done(((bf16[16,2,2,96,128]{4,3,2,1,0:T(8,128)(2,1)}), bf16[16,2,2,96,128]{4,3,2,1,0:T(8,128)(2,1)S(1)}, u32[]{:S(2)}, u32[]{:S(2)}) %all-to-all-start.4) | async-done | bytes 1572896 | tf_op jit(solution)/shard_map/all_to_all | solution.py:489
  196.2 1.1 copy-done.2
  197.3 7.3 %join.1 = bf16[3072,640]{1,0:T(8,128)(2,1)} custom-call(s32[5]{0:T(128)} %class_ref.17, s32[12,128]{1,0:T(8,128)} %bitcast.13, bf16[16,2,2,96,128]{4,3,2,1,0:T(8,128)(2,1)} %copy-done.2, bf16[3072,256]{1,0:T(8,128)(2,1)} %unpack.1.early_ref, bf16[3072,128]{1,0:T(8,128)(2,1)} %frame_attention.3.spatial_ref), custom_call_target="tpu_custom_call" | custom-call | flops 2415919104 | bytes 7864320 | tf_op jit(solution)/shard_map/join/pallas_call | solution.py:460
  (27 shorter events, 0.2 us)
Async XLA Ops:
  9.8 68.9 %all-to-all-start = ((bf16[16,4,2,96,128]{4,3,2,1,0:T(8,128)(2,1)}), bf16[16,4,2,96,128]{4,3,2,1,0:T(8,128)(2,1)S(1)}, u32[]{:S(2)}, u32[]{:S(2)}) async-start(bf16[16,4,2,96,128]{4,3,2,1,0:T(8,128)(2,1)} %pack_values.1), calls=%async_computation | async-start | bytes 6291456 | tf_op jit(solution)/shard_map/all_to_all | solution.py:489
  17.4 10.7 %copy-start.3 = (s32[5,12,12]{2,1,0:T(8,128)S(1)}, s32[5,12,12]{2,1,0:T(8,128)}, u32[]{:S(2)}) copy-start(s32[5,12,12]{2,1,0:T(8,128)} %param.15) | copy-start | bytes 8644
  17.4 10.7 %copy-start.5 = (f32[640]{0:T(1024)S(1)}, f32[640]{0:T(1024)}, u32[]{:S(2)}) copy-start(f32[640]{0:T(1024)} %param.13) | copy-start | bytes 7684
  17.5 10.7 %copy-start.6 = (f32[640]{0:T(1024)S(1)}, f32[640]{0:T(1024)}, u32[]{:S(2)}) copy-start(f32[640]{0:T(1024)} %param.12) | copy-start | bytes 7684
  23.7 2.0 collective-permute-start
  26.5 3.1 %collective-permute-start.1 = (f32[2,2,3,4,128]{4,3,2,1,0:T(4,128)S(1)}, f32[2,2,3,4,128]{4,3,2,1,0:T(4,128)S(1)}, u32[]{:S(2)}, u32[]{:S(2)}) collective-permute-start(f32[2,2,3,4,128]{4,3,2,1,0:T(4,128)S(1)} %add.15), channel_id=1, source_target_pairs={{0,2},{1,3},{2,0},{3,1},{4,6},{5,7},{6,4},{7,5},{8,10},{9,11},{10,... | collective-permute-start | bytes 73736 | tf_op jit(solution)/shard_map/ppermute | solution.py:497
  29.6 7.0 %collective-permute-start.2 = (f32[2,2,3,4,128]{4,3,2,1,0:T(4,128)S(1)}, f32[2,2,3,4,128]{4,3,2,1,0:T(4,128)S(1)}, u32[]{:S(2)}, u32[]{:S(2)}) collective-permute-start(f32[2,2,3,4,128]{4,3,2,1,0:T(4,128)S(1)} %add.16), channel_id=1, source_target_pairs={{0,4},{1,5},{2,6},{3,7},{4,0},{5,1},{6,2},{7,3},{8,12},{9,13},{10,... | collective-permute-start | bytes 73736 | tf_op jit(solution)/shard_map/ppermute | solution.py:497
  78.7 1.6 copy-start
  80.3 31.7 %all-to-all-start.1 = ((bf16[16,2,2,2,96,128]{5,4,3,2,1,0:T(8,128)(2,1)}), bf16[16,2,2,2,96,128]{5,4,3,2,1,0:T(8,128)(2,1)}, u32[]{:S(2)}, u32[]{:S(2)}) async-start(bf16[16,2,2,2,96,128]{5,4,3,2,1,0:T(8,128)(2,1)} %pack_norms.3), calls=%async_computation.1 | async-start | bytes 6291456 | tf_op jit(solution)/shard_map/all_to_all | solution.py:489
  95.0 25.6 %copy-start.4 = (s32[5,8,8]{2,1,0:T(8,128)S(1)}, s32[5,8,8]{2,1,0:T(8,128)}, u32[]{:S(2)}) copy-start(s32[5,8,8]{2,1,0:T(8,128)} %param.16) | copy-start | bytes 3844
  112.1 37.3 %all-to-all-start.2 = ((bf16[16,2,2,2,96,128]{5,4,3,2,1,0:T(8,128)(2,1)}), bf16[16,2,2,2,96,128]{5,4,3,2,1,0:T(8,128)(2,1)S(1)}, u32[]{:S(2)}, u32[]{:S(2)}) async-start(bf16[16,2,2,2,96,128]{5,4,3,2,1,0:T(8,128)(2,1)} %pack_norms.5), calls=%async_computation.2 | async-start | bytes 6291456 | tf_op jit(solution)/shard_map/all_to_all | solution.py:489
  149.4 8.4 %copy-start.1 = (bf16[16,2,2,2,96,128]{5,4,3,2,1,0:T(8,128)(2,1)}, bf16[16,2,2,2,96,128]{5,4,3,2,1,0:T(8,128)(2,1)S(1)}, u32[]{:S(2)}) copy-start(bf16[16,2,2,2,96,128]{5,4,3,2,1,0:T(8,128)(2,1)S(1)} %all-to-all-done.2.q_ref.k_ref) | copy-start | bytes 9437188
  149.4 24.3 %all-to-all-start.3 = ((bf16[16,2,2,96,128]{4,3,2,1,0:T(8,128)(2,1)}), bf16[16,2,2,96,128]{4,3,2,1,0:T(8,128)(2,1)}, u32[]{:S(2)}, u32[]{:S(2)}) async-start(bf16[16,2,2,96,128]{4,3,2,1,0:T(8,128)(2,1)} %window_attention.2), calls=%async_computation.3 | async-start | bytes 3145728 | tf_op jit(solution)/shard_map/all_to_all | solution.py:489
  173.7 22.5 %all-to-all-start.4 = ((bf16[16,2,2,96,128]{4,3,2,1,0:T(8,128)(2,1)}), bf16[16,2,2,96,128]{4,3,2,1,0:T(8,128)(2,1)S(1)}, u32[]{:S(2)}, u32[]{:S(2)}) async-start(bf16[16,2,2,96,128]{4,3,2,1,0:T(8,128)(2,1)} %window_attention.3), calls=%async_computation.4 | async-start | bytes 3145728 | tf_op jit(solution)/shard_map/all_to_all | solution.py:489
  196.2 1.1 copy-start.2

commit v3 on v1

v3 whole, which is shorter than its diff:
```python
import functools

import jax
import jax.numpy as jnp
from jax import lax
from jax.experimental import pallas as pl
from jax.experimental.pallas import tpu as pltpu
from jax.sharding import PartitionSpec as P

HEADS = 40
HEAD_DIM = 128
LOCATIONS = 1536
BLOCK = 128
WINDOW_SPAN = 32
GROUP = 5
TEMPORAL = 4
FEATURES = HEADS * HEAD_DIM
EPSILON = 1e-06
MASKED = -(2.0**100)
EXP2_SCALE = 1.4426950408889634 * HEAD_DIM ** (-0.5)
LANE_BLOCKS = LOCATIONS // 128
PAIR = 2
VMEM_LIMIT = 52 * 2**20

F32 = jnp.float32
BF16 = jnp.bfloat16


def params(vmem=VMEM_LIMIT):
    return pltpu.CompilerParams(vmem_limit_bytes=vmem)


def cost(flops, nbytes, exps=0):
    return pl.CostEstimate(flops=int(flops), bytes_accessed=int(nbytes), transcendentals=int(exps))


def spatial_head(class_ref):
    found = jnp.int32(0)
    for i in range(1, GROUP):
        found = found + i * (1 - class_ref[i])
    return found


def temporal_head(class_ref, j):
    return j + (j >= spatial_head(class_ref)).astype(jnp.int32)


def column(row):
    return jnp.broadcast_to(row, (128, 128)).T


def sums_kernel(q_ref, k_ref, out_ref):
    for a, ref in enumerate((q_ref, k_ref)):
        for i in range(q_ref.shape[0] // 128):
            part = jnp.zeros((128, 128), F32)
            for j in range(GROUP):
                x = ref[128 * i : 128 * i + 128, 128 * j : 128 * j + 128].astype(F32)
                part = part + x * x
            out_ref[a, 0, i, :] = jnp.sum(part.T, axis=0)


def square_sums(query_proj, key_proj):
    tokens, features = query_proj.shape
    frames = tokens // LOCATIONS
    in_spec = pl.BlockSpec((LOCATIONS, features), lambda f: (f, 0))
    return pl.pallas_call(
        sums_kernel,
        grid=(frames,),
        in_specs=[in_spec, in_spec],
        out_specs=pl.BlockSpec((2, 1, LANE_BLOCKS, 128), lambda f: (0, f, 0, 0)),
        out_shape=jax.ShapeDtypeStruct((2, frames, LANE_BLOCKS, 128), F32),
        compiler_params=params(),
        cost_estimate=cost(4 * tokens * features, 4 * tokens * features),
        name="square_sums",
    )(query_proj, key_proj)


def build_picked(order_ref, picked_ref):
    lanes = lax.broadcasted_iota(jnp.int32, (128, 128), 1).astype(F32)

    def body(i, carry):
        wanted = column(order_ref[pl.ds(i, 1), :].astype(F32))
        rows = pl.ds(pl.multiple_of(i * 128, 128), 128)
        for j in range(LANE_BLOCKS):
            hit = wanted == lanes + float(128 * j)
            picked_ref[rows, 128 * j : 128 * j + 128] = jnp.where(hit, 1.0, 0.0).astype(BF16)
        return carry

    lax.fori_loop(0, LANE_BLOCKS, body, 0)


def pick_rows(picked_ref, heads, store):
    rows = 384
    for c in range(LOCATIONS // rows):
        y = jnp.dot(
            picked_ref[rows * c : rows * c + rows, :], heads, preferred_element_type=F32
        ).astype(BF16)
        store(c, rows, y)


def factor_of(sums):
    return lax.rsqrt(sums * (1.0 / FEATURES) + EPSILON)


def norm_steps(first, class_ref, sums_ref, gain_ref, x_refs, out_ref, scratch):
    picked_ref, heads_ref, in_ref, packed_ref, in_sem, out_sem = scratch
    frames = sums_ref.shape[1]
    steps = 2 * frames

    def head(j):
        return pl.multiple_of(temporal_head(class_ref, first + j) * 128, 128)

    def fetch(x_ref, f, n, j):
        return pltpu.make_async_copy(
            x_ref.at[pl.ds(pl.multiple_of(LOCATIONS * f, LOCATIONS), LOCATIONS), pl.ds(head(j), 128)],
            in_ref.at[n * PAIR + j],
            in_sem.at[n * PAIR + j],
        )

    def send(n):
        return pltpu.make_async_copy(
            packed_ref.at[n], out_ref.at[:, :, n // frames, n % frames], out_sem.at[n]
        )

    def arrived(n):
        for j in range(PAIR):
            fetch(x_refs[0], n % frames, n, j).wait()

    def scale(n, i):
        factor = column(factor_of(sums_ref[n // frames, n % frames, i : i + 1, :]))
        rows = slice(128 * i, 128 * i + 128)
        for j in range(PAIR):
            x = in_ref[n * PAIR + j, rows, :].astype(F32)
            gain = gain_ref[n // frames, :, pl.ds(head(j), 128)]
            heads_ref[n % 2, rows, 128 * j : 128 * j + 128] = (x * factor * gain).astype(BF16)

    def products_of(n, also):
        def store(c, rows, y):
            slots = rows // 96
            for j in range(PAIR):
                packed_ref[n, slots * c : slots * c + slots, j] = y[
                    :, 128 * j : 128 * j + 128
                ].reshape(slots, 96, 128)
            if also:
                for i in range(rows * c // 128, rows * (c + 1) // 128):
                    scale(n + 1, i)

        pick_rows(picked_ref, heads_ref[n % 2], store)
        send(n).start()

    def body(n, carry):
        arrived(n + 1)
        products_of(n, True)
        return carry

    for n in range(steps):
        for j in range(PAIR):
            fetch(x_refs[n // frames], n % frames, n, j).start()
    arrived(0)
    for i in range(LANE_BLOCKS):
        scale(0, i)
    lax.fori_loop(0, steps - 1, body, 0)
    products_of(steps - 1, False)
    for n in range(steps):
        send(n).wait()


def pack_norm_kernel(
    first, class_ref, turn_ref, order_ref, sums_ref, gain_ref, q_ref, k_ref, *rest
):
    @pl.when(turn_ref[0] != 0)
    def _():
        build_picked(order_ref, rest[-6])
        norm_steps(first, class_ref, sums_ref, gain_ref, (q_ref, k_ref), rest[-7], rest[-6:])


def front_kernel(
    class_ref, odd_ref, order_ref, sums_ref, gain_ref, q_ref, k_ref, v_ref, *rest
):
    norm_ref, out_ref = rest[:2]
    scratch, (v_in_ref, v_packed_ref, v_in_sem, v_out_sem) = rest[2:8], rest[8:]
    picked_ref = scratch[0]
    frames = sums_ref.shape[1]
    rows = 384
    chunks = LOCATIONS // rows
    slots = rows // 96

    def fetch(f, j):
        h = pl.multiple_of(temporal_head(class_ref, j) * 128, 128)
        return pltpu.make_async_copy(
            v_ref.at[pl.ds(LOCATIONS * f, LOCATIONS), pl.ds(h, 128)],
            v_in_ref.at[f, :, pl.ds(128 * j, 128)],
            v_in_sem.at[f * TEMPORAL + j],
        )

    def send(f, c):
        return pltpu.make_async_copy(
            v_packed_ref.at[f, pl.ds(slots * c, slots)],
            out_ref.at[pl.ds(slots * c, slots), :, f],
            v_out_sem.at[f * chunks + c],
        )

    for f in range(frames):
        for j in range(TEMPORAL):
            fetch(f, j).start()

    build_picked(order_ref, picked_ref)

    @pl.when(odd_ref[0] != 0)
    def _():
        norm_steps(0, class_ref, sums_ref, gain_ref, (q_ref, k_ref), norm_ref, scratch)

    for f in range(frames):
        for j in range(TEMPORAL):
            fetch(f, j).wait()

        def store(c, rows, y):
            for j in range(TEMPORAL):
                v_packed_ref[f, slots * c : slots * c + slots, j] = y[
                    :, 128 * j : 128 * j + 128
                ].reshape(slots, 96, 128)
            send(f, c).start()

        pick_rows(picked_ref, v_in_ref[f], store)
    for f in range(frames):
        for c in range(chunks):
            send(f, c).wait()


def pack_specs(frames, features):
    anywhere = pl.BlockSpec(memory_space=pl.ANY)
    in_specs = [
        pl.BlockSpec((LANE_BLOCKS, 128), lambda i, c, t: (0, 0)),
        pl.BlockSpec((2, frames, LANE_BLOCKS, 128), lambda i, c, t: (0, 0, 0, 0)),
        pl.BlockSpec((2, 1, features), lambda i, c, t: (0, 0, 0)),
        anywhere,
        anywhere,
    ]
    scratch = [
        pltpu.VMEM((LOCATIONS, LOCATIONS), BF16),
        pltpu.VMEM((2, LOCATIONS, PAIR * 128), BF16),
        pltpu.VMEM((2 * frames * PAIR, LOCATIONS, 128), BF16),
        pltpu.VMEM((2 * frames, 16, PAIR, 96, 128), BF16),
        pltpu.SemaphoreType.DMA((2 * frames * PAIR,)),
        pltpu.SemaphoreType.DMA((2 * frames,)),
    ]
    norms = jax.ShapeDtypeStruct((16, PAIR, 2, frames, 96, 128), BF16)
    return in_specs, scratch, norms, anywhere


def pack_front(query_proj, key_proj, value_proj, sums, gains, head_class, order, odd):
    tokens, features = query_proj.shape
    frames = tokens // LOCATIONS
    in_specs, scratch, norms, anywhere = pack_specs(frames, features)
    chunks = LOCATIONS // 384
    return pl.pallas_call(
        front_kernel,
        grid_spec=pltpu.PrefetchScalarGridSpec(
            num_scalar_prefetch=2,
            grid=(1,),
            in_specs=[*in_specs, anywhere],
            out_specs=[anywhere, anywhere],
            scratch_shapes=[
                *scratch,
                pltpu.VMEM((frames, LOCATIONS, TEMPORAL * 128), BF16),
                pltpu.VMEM((frames, 16, TEMPORAL, 96, 128), BF16),
                pltpu.SemaphoreType.DMA((frames * TEMPORAL,)),
                pltpu.SemaphoreType.DMA((frames * chunks,)),
            ],
        ),
        out_shape=[norms, jax.ShapeDtypeStruct((16, TEMPORAL, frames, 96, 128), BF16)],
        compiler_params=params(),
        cost_estimate=cost(6 * tokens * LOCATIONS * 256, 12 * tokens * 256),
        name="pack_front",
    )(head_class, odd, order, sums, gains, query_proj, key_proj, value_proj)


def pack_norms(query_proj, key_proj, sums, gains, head_class, order, first, turn, before=None):
    tokens, features = query_proj.shape
    frames = tokens // LOCATIONS
    in_specs, scratch, norms, anywhere = pack_specs(frames, features)
    operands = [head_class, turn, order, sums, gains, query_proj, key_proj]
    aliases = {}
    if before is not None:
        in_specs.append(anywhere)
        aliases = {len(operands): 0}
        operands.append(before)
    return pl.pallas_call(
        functools.partial(pack_norm_kernel, first),
        grid_spec=pltpu.PrefetchScalarGridSpec(
            num_scalar_prefetch=2,
            grid=(1,),
            in_specs=in_specs,
            out_specs=anywhere,
            scratch_shapes=scratch,
        ),
        out_shape=norms,
        input_output_aliases=aliases,
        compiler_params=params(),
        cost_estimate=cost(4 * tokens * LOCATIONS * 256, 8 * tokens * 256),
        name="pack_norms",
    )(*operands)


def attend(count, scores, values, store):
    s = scores(0)
    for c in range(count):
        later = scores(c + 1) if c + 1 < count else None
        top = jnp.max(s, axis=1, keepdims=True)
        w = jnp.exp2((s - top) * EXP2_SCALE)
        total = jnp.sum(w, axis=1, keepdims=True)
        mixture = jnp.dot(w.astype(BF16), values(c), preferred_element_type=F32)
        store(c, (mixture / total).astype(BF16))
        s = later


def products(queries, key_rows):
    return lax.dot_general(
        queries, key_rows, (((1,), (1,)), ((), ())), preferred_element_type=F32
    )


def window_kernel(class_ref, bias_ref, q_ref, k_ref, v_ref, *rest):
    out_ref, wide_q_ref, wide_k_ref = rest[-3:]
    tokens = 16 * 2 * WINDOW_SPAN
    windows = 96 // WINDOW_SPAN

    @pl.when(pl.program_id(0) == 0)
    def _():
        place = lax.broadcasted_iota(jnp.int32, (tokens, 128), 0) % WINDOW_SPAN
        lane = lax.broadcasted_iota(jnp.int32, (tokens, 128), 1)
        own = jnp.where(place // 4 == lane, 1.0, 0.0).astype(BF16)
        for w in range(windows):
            wide_q_ref[w, :, 128:] = own

    repeated = jnp.broadcast_to(bias_ref[...], (32, WINDOW_SPAN, 128))
    repeated = repeated.reshape(tokens, 128).astype(BF16)
    for w in range(windows):
        rows = slice(WINDOW_SPAN * w, WINDOW_SPAN * w + WINDOW_SPAN)
        wide_q_ref[w, :, :128] = q_ref[:, 0, 0, :, rows, :].reshape(tokens, 128)
        wide_k_ref[w, :, :128] = k_ref[:, 0, 0, :, rows, :].reshape(tokens, 128)
        wide_k_ref[w, :, 128:] = repeated

    rows = 256
    parts = tokens // rows

    def scores(c):
        w, r = divmod(c, parts)
        return products(wide_q_ref[w, rows * r : rows * r + rows, :], wide_k_ref[w])

    def values(c):
        w = c // parts
        return v_ref[:, 0, :, WINDOW_SPAN * w : WINDOW_SPAN * w + WINDOW_SPAN, :].reshape(
            tokens, 128
        )

    def store(c, o):
        w, r = divmod(c, parts)
        slots = rows // (2 * WINDOW_SPAN)
        out_ref[
            slots * r : slots * r + slots, 0, :, WINDOW_SPAN * w : WINDOW_SPAN * w + WINDOW_SPAN, :
        ] = o.reshape(slots, 2, WINDOW_SPAN, 128)

    attend(windows * parts, scores, values, store)


def window_attention(moved, values, bias, head_class, first, before=None):
    count = moved.shape[1]
    windows = 96 // WINDOW_SPAN
    tokens = 16 * 2 * WINDOW_SPAN
    qk_block = (16, 1, 1, 2, 96, 128)
    in_specs = [
        pl.BlockSpec((1, WINDOW_SPAN, 128), lambda h, c: (temporal_head(c, h + first), 0, 0)),
        pl.BlockSpec(qk_block, lambda h, c: (0, h, 0, 0, 0, 0)),
        pl.BlockSpec(qk_block, lambda h, c: (0, h, 1, 0, 0, 0)),
        pl.BlockSpec((16, 1, 2, 96, 128), lambda h, c: (0, h + first, 0, 0, 0)),
    ]
    operands = [head_class, bias, moved, moved, values]
    aliases = {}
    if before is not None:
        in_specs.append(pl.BlockSpec(memory_space=pl.ANY))
        aliases = {len(operands): 0}
        operands.append(before)
    return pl.pallas_call(
        window_kernel,
        grid_spec=pltpu.PrefetchScalarGridSpec(
            num_scalar_prefetch=1,
            grid=(count,),
            in_specs=in_specs,
            out_specs=pl.BlockSpec((16, 1, 2, 96, 128), lambda h, c: (0, h + first, 0, 0, 0)),
            scratch_shapes=[
                pltpu.VMEM((windows, tokens, 256), BF16),
                pltpu.VMEM((windows, tokens, 256), BF16),
            ],
        ),
        out_shape=jax.ShapeDtypeStruct((16, TEMPORAL, 2, 96, 128), BF16),
        input_output_aliases=aliases,
        compiler_params=params(),
        cost_estimate=cost(
            8 * count * windows * tokens * tokens * 128,
            8 * count * windows * tokens * 128,
            count * windows * tokens * tokens,
        ),
        name="window_attention",
    )(*operands)


def frame_kernel(
    class_ref, bias_ref, sums_ref, qg_ref, kg_ref, q_ref, k_ref, v_ref, out_ref, wide_q_ref, wide_k_ref
):
    lane = lax.broadcasted_iota(jnp.int32, (128, 128), 1)
    streams = ((q_ref, qg_ref, wide_q_ref), (k_ref, kg_ref, wide_k_ref))
    for a, (x_ref, gain_ref, wide_ref) in enumerate(streams):
        factor = factor_of(sums_ref[a, 0])
        for i in range(LANE_BLOCKS):
            rows = slice(128 * i, 128 * i + 128)
            x = x_ref[rows, :].astype(F32)
            wide_ref[rows, :128] = (x * column(factor[i : i + 1, :]) * gain_ref[0]).astype(BF16)
            if a == 0:
                extra = jnp.where(lane == i, 1.0, 0.0)
            else:
                extra = jnp.broadcast_to(bias_ref[0, i : i + 1, :], (128, 128))
            wide_ref[rows, 128:] = extra.astype(BF16)

    rows = 256

    def scores(c):
        return products(wide_q_ref[rows * c : rows * c + rows, :], wide_k_ref[...])

    def store(c, o):
        out_ref[rows * c : rows * c + rows, :] = o

    attend(LOCATIONS // rows, scores, lambda c: v_ref[...], store)


def frame_attention(query_proj, key_proj, value_proj, sums, gains, bias, head_class):
    tokens = query_proj.shape[0]
    frames = tokens // LOCATIONS
    column_spec = pl.BlockSpec((LOCATIONS, 128), lambda f, c: (f, spatial_head(c)))
    return pl.pallas_call(
        frame_kernel,
        grid_spec=pltpu.PrefetchScalarGridSpec(
            num_scalar_prefetch=1,
            grid=(frames,),
            in_specs=[
                pl.BlockSpec((1, LANE_BLOCKS, 128), lambda f, c: (spatial_head(c), 0, 0)),
                pl.BlockSpec((2, 1, LANE_BLOCKS, 128), lambda f, c: (0, f, 0, 0)),
                pl.BlockSpec((1, 1, 128), lambda f, c: (0, 0, spatial_head(c))),
                pl.BlockSpec((1, 1, 128), lambda f, c: (1, 0, spatial_head(c))),
                column_spec,
                column_spec,
                column_spec,
            ],
            out_specs=pl.BlockSpec((LOCATIONS, 128), lambda f, c: (f, 0)),
            scratch_shapes=[
                pltpu.VMEM((LOCATIONS, 256), BF16),
                pltpu.VMEM((LOCATIONS, 256), BF16),
            ],
        ),
        out_shape=jax.ShapeDtypeStruct((tokens, 128), BF16),
        compiler_params=params(),
        cost_estimate=cost(
            4 * tokens * LOCATIONS * 256, 8 * tokens * 128, tokens * LOCATIONS
        ),
        name="frame_attention",
    )(head_class, bias, sums, gains, gains, query_proj, key_proj, value_proj)


def place_rows(order_ref, moved_ref, heads_ref, rows):
    count, frames = moved_ref.shape[1:3]

    @pl.when(pl.program_id(0) == 0)
    def _():
        for f in range(frames):
            for j in range(count):
                at = 128 * (f * count + j)
                heads_ref[:, at : at + 128] = moved_ref[:, j, f].reshape(LOCATIONS, 128)

    places = lax.broadcasted_iota(jnp.int32, (rows, 128), 0) + pl.program_id(0) * rows
    parts = []
    for i in range(LANE_BLOCKS):
        hit = order_ref[i : i + 1, :] == places
        parts.append(jnp.where(hit, 1.0, 0.0).astype(BF16))
    return jnp.dot(
        jnp.concatenate(parts, axis=1), heads_ref[...], preferred_element_type=F32
    ).astype(BF16)


def join_kernel(class_ref, order_ref, moved_ref, spatial_ref, out_ref, heads_ref):
    frames, rows = out_ref.shape[:2]
    y = place_rows(order_ref, moved_ref, heads_ref, rows)
    for f in range(frames):
        for j in range(TEMPORAL):
            h = pl.multiple_of(temporal_head(class_ref, j) * 128, 128)
            at = 128 * (f * TEMPORAL + j)
            out_ref[f, :, pl.ds(h, 128)] = y[:, at : at + 128]
        h = pl.multiple_of(spatial_head(class_ref) * 128, 128)
        out_ref[f, :, pl.ds(h, 128)] = spatial_ref[f]


def join(returned, spatial_out, head_class, order):
    count, frames = returned.shape[1:3]
    rows = 384
    width = GROUP * 128
    joined = pl.pallas_call(
        join_kernel,
        grid_spec=pltpu.PrefetchScalarGridSpec(
            num_scalar_prefetch=1,
            grid=(LOCATIONS // rows,),
            in_specs=[
                pl.BlockSpec((LANE_BLOCKS, 128), lambda i, c: (0, 0)),
                pl.BlockSpec((16, count, frames, 96, 128), lambda i, c: (0, 0, 0, 0, 0)),
                pl.BlockSpec((frames, rows, 128), lambda i, c: (0, i, 0)),
            ],
            out_specs=pl.BlockSpec((frames, rows, width), lambda i, c: (0, i, 0)),
            scratch_shapes=[pltpu.VMEM((LOCATIONS, frames * count * 128), BF16)],
        ),
        out_shape=jax.ShapeDtypeStruct((frames, LOCATIONS, width), BF16),
        compiler_params=params(),
        cost_estimate=cost(
            2 * frames * LOCATIONS * LOCATIONS * 128 * count, 4 * frames * LOCATIONS * width
        ),
        name="join",
    )(head_class, order, returned, spatial_out.reshape(frames, LOCATIONS, 128))
    return joined.reshape(frames * LOCATIONS, width)


def key_bias(mask):
    blocks = mask.shape[-1]
    same = jnp.arange(blocks)[:, None] == jnp.arange(blocks)[None, :]
    bias = jnp.where((mask != 0) | same, 0.0, MASKED).astype(F32)
    return jnp.pad(jnp.swapaxes(bias, 1, 2), ((0, 0), (0, 0), (0, 128 - blocks)))


def exchange(tensor):
    return lax.all_to_all(tensor, "seq", split_axis=0, concat_axis=0, tiled=True)


def butterfly(sums, step, keep=lambda i: True):
    pairs = [(i, i ^ step) for i in range(lax.axis_size("head")) if keep(i)]
    return sums + lax.ppermute(sums, "head", pairs)


def shards(
    query_proj,
    key_proj,
    value_proj,
    query_gain,
    key_gain,
    head_class,
    spatial_mask,
    temporal_mask,
    location_order,
):
    order = location_order.reshape(LANE_BLOCKS, 128)
    gains = jnp.stack([query_gain, key_gain])[:, None, :]
    window_bias = jnp.repeat(key_bias(temporal_mask), 4, axis=1)
    frame_bias = key_bias(spatial_mask)
    odd = (lax.axis_index("head") % 2).astype(jnp.int32).reshape(1)

    def norms(first, turn, before=None):
        return pack_norms(
            query_proj, key_proj, sums, gains, head_class, order, first, turn, before
        )

    sums = butterfly(square_sums(query_proj, key_proj), 1)
    for step in (2, 4):
        sums = butterfly(sums, step, lambda i: i % 2 == 1)
    first, packed_values = pack_front(
        query_proj, key_proj, value_proj, sums, gains, head_class, order, odd
    )
    packed_values, first, sums = lax.optimization_barrier((packed_values, first, sums))

    values = exchange(packed_values)
    for step in (2, 4):
        sums = butterfly(sums, step, lambda i: i % 2 == 0)
    first = norms(0, 1 - odd, first)
    values, first = lax.optimization_barrier((values, first))

    moved = exchange(first)
    second = norms(PAIR, jnp.ones((1,), jnp.int32))
    spatial_out = frame_attention(
        query_proj, key_proj, value_proj, sums, gains, frame_bias, head_class
    )
    moved, spatial_out, second = lax.optimization_barrier((moved, spatial_out, second))

    moved_later = exchange(second)
    mixed = window_attention(moved, values, window_bias, head_class, 0)
    mixed, moved_later = lax.optimization_barrier((mixed, moved_later))

    mixed = window_attention(moved_later, values, window_bias, head_class, PAIR, mixed)
    return join(exchange(mixed), spatial_out, head_class, order)


def solution(mesh):
    return jax.shard_map(
        shards,
        mesh=mesh,
        in_specs=(
            P("seq", "head"),
            P("seq", "head"),
            P("seq", "head"),
            P("head"),
            P("head"),
            P("head"),
            P("head", None, None),
            P("head", None, None),
            P(),
        ),
        out_specs=P("seq", "head"),
        check_vma=False,
    )
```

time: 252 us -> 199 us (0.79)
  the two profiles are of different devices: /device:TPU:96 before, /device:TPU:1 now
where the time goes in v3:
time: 199 us; the launch traced here: 198 us
  Pallas kernels  74.6 us (37%)
  waiting for transfers between devices  51.6 us (26%)
  starting transfers between devices  35.4 us (18%)
  blocking collectives  34.3 us (17%)
    all_to_all x3, waiting for transfers between devices, exchange(): lax.all_to_all(tensor, 'seq', split_axis=0, concat_axis=0, tiled=True)  48.2 us
    all_to_all x1, blocking collectives, exchange(): lax.all_to_all(tensor, 'seq', split_axis=0, concat_axis=0, tiled=True)  34.3 us
    pallas_call x2, Pallas kernels, window_attention(): pl.pallas_call(window_kernel, grid_spec=pltpu.PrefetchScalarGridSpec(num_...  23.8 us
    all_to_all x3, starting transfers between devices, exchange(): lax.all_to_all(tensor, 'seq', split_axis=0, concat_axis=0, tiled=True)  23.7 us
    pallas_call x1, Pallas kernels, pack_front(): pl.pallas_call(front_kernel, grid_spec=pltpu.PrefetchScalarGridSpec(num_s...  16.6 us
    ppermute x5, starting transfers between devices, butterfly(): return sums + lax.ppermute(sums, 'head', pairs)  11.8 us
    pallas_call x2, Pallas kernels, pack_norms(): pl.pallas_call(functools.partial(pack_norm_kernel, first), grid_spec=pltp...  11 us
    pallas_call x1, Pallas kernels, join(): pl.pallas_call(join_kernel, grid_spec=pltpu.PrefetchScalarGridSpec(num_sc...  10.2 us
  transfers between devices with their start and end apart: 8, of which 6 were waited for; matrix products, arithmetic and copies ran while one was open for 0% of the time, Pallas kernels for 16%

profile of v3, /device:TPU:1, one launch (start us, length us, event | category | flops | bytes accessed | tf_op | source)
XLA Modules:
  0.0 198.2 jit_solution(8506629737994131804)
XLA Ops:
  0.0 4.2 %square_sums.1 = f32[2,2,12,128]{3,2,1,0:T(8,128)S(1)} custom-call(bf16[3072,640]{1,0:T(8,128)(2,1)} %q_ref.9, bf16[3072,640]{1,0:T(8,128)(2,1)} %k_ref.9), custom_call_target="tpu_custom_call" | custom-call | flops 7864320 | bytes 7864320 | tf_op jit(solution)/shard_map/square_sums/pallas_call | solution.py:66
  4.2 1.5 collective-permute-start
  5.7 0.9 collective-permute-done
  6.6 3.6 %collective-permute-start.1 = (f32[2,2,12,128]{3,2,1,0:T(8,128)S(1)}, f32[2,2,12,128]{3,2,1,0:T(8,128)S(1)}, u32[]{:S(2)}, u32[]{:S(2)}) collective-permute-start(f32[2,2,12,128]{3,2,1,0:T(8,128)S(1)} %add.24), channel_id=1, source_target_pairs={{1,3},{3,1},{5,7},{7,5},{9,11},{11,9},{13,15},{15,13},{17,19},{19,... | collective-permute-start | bytes 73736 | tf_op jit(solution)/shard_map/ppermute | solution.py:541
  10.3 1.2 collective-permute-done.1
  11.5 5.3 %collective-permute-start.2 = (f32[2,2,12,128]{3,2,1,0:T(8,128)S(1)}, f32[2,2,12,128]{3,2,1,0:T(8,128)S(1)}, u32[]{:S(2)}, u32[]{:S(2)}) collective-permute-start(f32[2,2,12,128]{3,2,1,0:T(8,128)S(1)} %add.25), channel_id=1, source_target_pairs={{1,5},{3,7},{5,1},{7,3},{9,13},{11,15},{13,9},{15,11},{17,21},{19,... | collective-permute-start | bytes 73736 | tf_op jit(solution)/shard_map/ppermute | solution.py:541
  16.9 1.2 collective-permute-done.2
  18.1 0.0 copy-done
  18.1 16.6 %pack_front.1 = (bf16[16,2,2,2,96,128]{5,4,3,2,1,0:T(8,128)(2,1)}, bf16[16,4,2,96,128]{4,3,2,1,0:T(8,128)(2,1)}) custom-call(s32[5]{0:T(128)S(1)} %copy-done.1, s32[1]{0:T(128)} %bitcast.3.odd_ref, s32[12,128]{1,0:T(8,128)S(1)} %bitcast.11, f32[2,2,12,128]{3,2,1,0:T(8,128)S(1)} %add.26.sums_ref, f32[2,1,640]{2,1,0:T(1,128)S(1)} %broadcast_in_dim.31.gain_ref.qg_ref.kg_ref, ...), custom_call_target="tpu_custom_call" | custom-call | flops 7247757312 | bytes 9437184 | tf_op jit(solution)/shard_map/pack_front/pallas_call | solution.py:256
  34.7 6.8 %all-to-all-start = ((bf16[16,4,2,96,128]{4,3,2,1,0:T(8,128)(2,1)}), bf16[16,4,2,96,128]{4,3,2,1,0:T(8,128)(2,1)S(1)}, u32[]{:S(2)}, u32[]{:S(2)}) async-start(bf16[16,4,2,96,128]{4,3,2,1,0:T(8,128)(2,1)} %get-tuple-element.19), calls=%async_computation | async-start | bytes 6291456 | tf_op jit(solution)/shard_map/all_to_all | solution.py:536
  41.5 0.7 collective-permute-start.3
  42.2 0.0 collective-permute-done.3
  42.2 0.7 collective-permute-start.4
  42.9 0.0 collective-permute-done.4
  42.9 0.7 pack_norms.2
  43.6 0.0 copy-start.3
  43.6 25.0 %all-to-all-done.v_ref = bf16[16,4,2,96,128]{4,3,2,1,0:T(8,128)(2,1)S(1)} async-done(((bf16[16,4,2,96,128]{4,3,2,1,0:T(8,128)(2,1)}), bf16[16,4,2,96,128]{4,3,2,1,0:T(8,128)(2,1)S(1)}, u32[]{:S(2)}, u32[]{:S(2)}) %all-to-all-start) | async-done | bytes 3145760 | tf_op jit(solution)/shard_map/all_to_all | solution.py:536
  68.6 1.6 copy-done.2
  70.2 8.5 %all-to-all-start.1 = ((bf16[16,2,2,2,96,128]{5,4,3,2,1,0:T(8,128)(2,1)}), bf16[16,2,2,2,96,128]{5,4,3,2,1,0:T(8,128)(2,1)}, u32[]{:S(2)}, u32[]{:S(2)}) async-start(bf16[16,2,2,2,96,128]{5,4,3,2,1,0:T(8,128)(2,1)} %pack_norms.2), calls=%async_computation.1 | async-start | bytes 6291456 | tf_op jit(solution)/shard_map/all_to_all | solution.py:536
  78.7 0.1 copy.13
  78.9 10.3 %pack_norms.3 = bf16[16,2,2,2,96,128]{5,4,3,2,1,0:T(8,128)(2,1)} custom-call(s32[5]{0:T(128)S(1)} %copy-done.1, s32[1]{0:T(128)} %constant.26.clone.1.turn_ref, s32[12,128]{1,0:T(8,128)S(1)} %bitcast.13, f32[2,2,12,128]{3,2,1,0:T(8,128)S(1)} %add.28.sums_ref, f32[2,1,640]{2,1,0:T(1,128)S(1)} %broadcast_in_dim.31.gain_ref.qg_ref.kg_ref, ...), custom_call_target="tpu_custom_call" | custom-call | flops 4831838208 | bytes 6291456 | tf_op jit(solution)/shard_map/pack_norms/pallas_call | solution.py:288
  89.2 8.9 %frame_attention.1 = bf16[3072,128]{1,0:T(8,128)(2,1)S(1)} custom-call(s32[5]{0:T(128)S(1)} %copy-done.1, f32[5,12,128]{2,1,0:T(8,128)S(1)} %pad.9.bias_ref, f32[2,2,12,128]{3,2,1,0:T(8,128)S(1)} %add.28.sums_ref, f32[2,1,640]{2,1,0:T(1,128)S(1)} %broadcast_in_dim.31.gain_ref.qg_ref.kg_ref, f32[2,1,640]{2,1,0:T(1,128)S(1)} %broadcast_in_dim.31.gain_ref.qg_ref.kg_ref, ...), custom_call_target="tpu_custom_call" | custom-call | flops 4831838208 | bytes 3145728 | tf_op jit(solution)/shard_map/frame_attention/pallas_call | solution.py:440
  98.1 0.0 copy-start.4
  98.1 9.1 %all-to-all-done.1.q_ref.k_ref = bf16[16,2,2,2,96,128]{5,4,3,2,1,0:T(8,128)(2,1)} async-done(((bf16[16,2,2,2,96,128]{5,4,3,2,1,0:T(8,128)(2,1)}), bf16[16,2,2,2,96,128]{5,4,3,2,1,0:T(8,128)(2,1)}, u32[]{:S(2)}, u32[]{:S(2)}) %all-to-all-start.1) | async-done | bytes 3145760 | tf_op jit(solution)/shard_map/all_to_all | solution.py:536
  107.2 8.4 %all-to-all-start.2 = ((bf16[16,2,2,2,96,128]{5,4,3,2,1,0:T(8,128)(2,1)}), bf16[16,2,2,2,96,128]{5,4,3,2,1,0:T(8,128)(2,1)}, u32[]{:S(2)}, u32[]{:S(2)}) async-start(bf16[16,2,2,2,96,128]{5,4,3,2,1,0:T(8,128)(2,1)} %pack_norms.3), calls=%async_computation.2 | async-start | bytes 6291456 | tf_op jit(solution)/shard_map/all_to_all | solution.py:536
  115.6 0.0 copy-done.4
  115.7 0.1 copy.14
  115.8 11.9 %window_attention.2.rest_0_ = bf16[16,4,2,96,128]{4,3,2,1,0:T(8,128)(2,1)} custom-call(s32[5]{0:T(128)S(1)} %copy-done.1, f32[5,32,128]{2,1,0:T(8,128)S(1)} %bitcast.9, bf16[16,2,2,2,96,128]{5,4,3,2,1,0:T(8,128)(2,1)} %all-to-all-done.1.q_ref.k_ref, bf16[16,2,2,2,96,128]{5,4,3,2,1,0:T(8,128)(2,1)} %all-to-all-done.1.q_ref.k_ref, ...), custom_call_target="tpu_custom_call" | custom-call | flops 6442450944 | bytes 6291456 | tf_op jit(solution)/shard_map/window_attention/pallas_call | solution.py:384
  127.7 14.2 %all-to-all-done.2.q_ref.k_ref = bf16[16,2,2,2,96,128]{5,4,3,2,1,0:T(8,128)(2,1)} async-done(((bf16[16,2,2,2,96,128]{5,4,3,2,1,0:T(8,128)(2,1)}), bf16[16,2,2,2,96,128]{5,4,3,2,1,0:T(8,128)(2,1)}, u32[]{:S(2)}, u32[]{:S(2)}) %all-to-all-start.2) | async-done | bytes 3145760 | tf_op jit(solution)/shard_map/all_to_all | solution.py:536
  141.8 11.9 %window_attention.3 = bf16[16,4,2,96,128]{4,3,2,1,0:T(8,128)(2,1)} custom-call(s32[5]{0:T(128)S(1)} %copy-done.1, f32[5,32,128]{2,1,0:T(8,128)S(1)} %bitcast.10, bf16[16,2,2,2,96,128]{5,4,3,2,1,0:T(8,128)(2,1)} %all-to-all-done.2.q_ref.k_ref, bf16[16,2,2,2,96,128]{5,4,3,2,1,0:T(8,128)(2,1)} %all-to-all-done.2.q_ref.k_ref, ...), custom_call_target="tpu_custom_call", output_to_operand_aliasing={{}: (5, {})} | custom-call | flops 6442450944 | bytes 6291456 | tf_op jit(solution)/shard_map/window_attention/pallas_call | solution.py:384
  153.7 34.3 %all_to_all.20.moved_ref = bf16[16,4,2,96,128]{4,3,2,1,0:T(8,128)(2,1)} all-to-all(bf16[16,4,2,96,128]{4,3,2,1,0:T(8,128)(2,1)} %window_attention.3), channel_id=1, replica_groups=mesh['seq'=16,'head'=8] {'seq'}, dimensions={0} | all-to-all | bytes 6291456 | tf_op jit(solution)/shard_map/all_to_all | solution.py:536
  188.1 10.2 %join.1 = bf16[2,1536,640]{2,1,0:T(8,128)(2,1)} custom-call(s32[5]{0:T(128)S(1)} %copy-done.1, s32[12,128]{1,0:T(8,128)S(1)} %bitcast.14, bf16[16,4,2,96,128]{4,3,2,1,0:T(8,128)(2,1)} %all_to_all.20.moved_ref, bf16[2,1536,128]{2,1,0:T(8,128)(2,1)S(1)} %bitcast.15), custom_call_target="tpu_custom_call" | custom-call | flops 4831838208 | bytes 7864320 | tf_op jit(solution)/shard_map/join/pallas_call | solution.py:505
  (25 shorter events, 0.1 us)
Async XLA Ops:
  0.0 10.2 %copy-start.5 = (f32[640]{0:T(1024)S(1)}, f32[640]{0:T(1024)}, u32[]{:S(2)}) copy-start(f32[640]{0:T(1024)} %param.12) | copy-start | bytes 7684
  0.0 10.2 %copy-start.6 = (f32[640]{0:T(1024)S(1)}, f32[640]{0:T(1024)}, u32[]{:S(2)}) copy-start(f32[640]{0:T(1024)} %param.13) | copy-start | bytes 7684
  0.0 18.1 %copy-start.1 = (s32[5]{0:T(128)S(1)}, s32[5]{0:T(128)}, u32[]{:S(2)}) copy-start(s32[5]{0:T(128)} %class_ref.13) | copy-start | bytes 64
  0.0 18.1 %copy-start = (s32[1536]{0:T(1024)S(1)}, s32[1536]{0:T(1024)}, u32[]{:S(2)}) copy-start(s32[1536]{0:T(1024)} %param.17) | copy-start | bytes 18436
  4.2 2.4 %collective-permute-start = (f32[2,2,12,128]{3,2,1,0:T(8,128)S(1)}, f32[2,2,12,128]{3,2,1,0:T(8,128)S(1)}, u32[]{:S(2)}, u32[]{:S(2)}) collective-permute-start(f32[2,2,12,128]{3,2,1,0:T(8,128)S(1)} %square_sums.1), channel_id=1, source_target_pairs={{0,1},{1,0},{2,3},{3,2},{4,5},{5,4},{6,7},{7,6},{8,9},{9,8},{10,11... | collective-permute-start | bytes 73736 | tf_op jit(solution)/shard_map/ppermute | solution.py:541
  6.6 4.9 %collective-permute-start.1 = (f32[2,2,12,128]{3,2,1,0:T(8,128)S(1)}, f32[2,2,12,128]{3,2,1,0:T(8,128)S(1)}, u32[]{:S(2)}, u32[]{:S(2)}) collective-permute-start(f32[2,2,12,128]{3,2,1,0:T(8,128)S(1)} %add.24), channel_id=1, source_target_pairs={{1,3},{3,1},{5,7},{7,5},{9,11},{11,9},{13,15},{15,13},{17,19},{19,... | collective-permute-start | bytes 73736 | tf_op jit(solution)/shard_map/ppermute | solution.py:541
  11.5 6.6 %collective-permute-start.2 = (f32[2,2,12,128]{3,2,1,0:T(8,128)S(1)}, f32[2,2,12,128]{3,2,1,0:T(8,128)S(1)}, u32[]{:S(2)}, u32[]{:S(2)}) collective-permute-start(f32[2,2,12,128]{3,2,1,0:T(8,128)S(1)} %add.25), channel_id=1, source_target_pairs={{1,5},{3,7},{5,1},{7,3},{9,13},{11,15},{13,9},{15,11},{17,21},{19,... | collective-permute-start | bytes 73736 | tf_op jit(solution)/shard_map/ppermute | solution.py:541
  34.7 33.8 %all-to-all-start = ((bf16[16,4,2,96,128]{4,3,2,1,0:T(8,128)(2,1)}), bf16[16,4,2,96,128]{4,3,2,1,0:T(8,128)(2,1)S(1)}, u32[]{:S(2)}, u32[]{:S(2)}) async-start(bf16[16,4,2,96,128]{4,3,2,1,0:T(8,128)(2,1)} %get-tuple-element.19), calls=%async_computation | async-start | bytes 6291456 | tf_op jit(solution)/shard_map/all_to_all | solution.py:536
  41.5 0.7 collective-permute-start.3
  42.2 0.7 collective-permute-start.4
  43.6 35.1 %copy-start.3 = (s32[5,12,12]{2,1,0:T(8,128)S(1)}, s32[5,12,12]{2,1,0:T(8,128)}, u32[]{:S(2)}) copy-start(s32[5,12,12]{2,1,0:T(8,128)} %param.15) | copy-start | bytes 8644
  68.5 1.6 copy-start.2
  70.2 37.0 %all-to-all-start.1 = ((bf16[16,2,2,2,96,128]{5,4,3,2,1,0:T(8,128)(2,1)}), bf16[16,2,2,2,96,128]{5,4,3,2,1,0:T(8,128)(2,1)}, u32[]{:S(2)}, u32[]{:S(2)}) async-start(bf16[16,2,2,2,96,128]{5,4,3,2,1,0:T(8,128)(2,1)} %pack_norms.2), calls=%async_computation.1 | async-start | bytes 6291456 | tf_op jit(solution)/shard_map/all_to_all | solution.py:536
  98.1 17.5 %copy-start.4 = (s32[5,8,8]{2,1,0:T(8,128)S(1)}, s32[5,8,8]{2,1,0:T(8,128)}, u32[]{:S(2)}) copy-start(s32[5,8,8]{2,1,0:T(8,128)} %param.16) | copy-start | bytes 3844
  107.2 34.6 %all-to-all-start.2 = ((bf16[16,2,2,2,96,128]{5,4,3,2,1,0:T(8,128)(2,1)}), bf16[16,2,2,2,96,128]{5,4,3,2,1,0:T(8,128)(2,1)}, u32[]{:S(2)}, u32[]{:S(2)}) async-start(bf16[16,2,2,2,96,128]{5,4,3,2,1,0:T(8,128)(2,1)} %pack_norms.3), calls=%async_computation.2 | async-start | bytes 6291456 | tf_op jit(solution)/shard_map/all_to_all | solution.py:536

commit v4 on v3

--- a/solution.py
+++ b/solution.py
@@ -20,7 +20,7 @@
 EXP2_SCALE = 1.4426950408889634 * HEAD_DIM ** (-0.5)
 LANE_BLOCKS = LOCATIONS // 128
 PAIR = 2
-VMEM_LIMIT = 52 * 2**20
+VMEM_LIMIT = 50 * 2**20
 
 F32 = jnp.float32
 BF16 = jnp.bfloat16
@@ -90,7 +90,7 @@
 
 
 def pick_rows(picked_ref, heads, store):
-    rows = 384
+    rows = 768
     for c in range(LOCATIONS // rows):
         y = jnp.dot(
             picked_ref[rows * c : rows * c + rows, :], heads, preferred_element_type=F32
@@ -181,7 +181,7 @@
     scratch, (v_in_ref, v_packed_ref, v_in_sem, v_out_sem) = rest[2:8], rest[8:]
     picked_ref = scratch[0]
     frames = sums_ref.shape[1]
-    rows = 384
+    rows = 768
     chunks = LOCATIONS // rows
     slots = rows // 96
 
@@ -252,7 +252,7 @@
     tokens, features = query_proj.shape
     frames = tokens // LOCATIONS
     in_specs, scratch, norms, anywhere = pack_specs(frames, features)
-    chunks = LOCATIONS // 384
+    chunks = LOCATIONS // 768
     return pl.pallas_call(
         front_kernel,
         grid_spec=pltpu.PrefetchScalarGridSpec(
@@ -500,7 +500,7 @@
 
 def join(returned, spatial_out, head_class, order):
     count, frames = returned.shape[1:3]
-    rows = 384
+    rows = 768
     width = GROUP * 128
     joined = pl.pallas_call(
         join_kernel,

time: 199 us -> 199 us (level)
  Pallas kernels: 74.6 us -> 70.1 us
  blocking collectives: 34.3 us -> 37.2 us
  local copies, waits for them, and re-layouts: 1.91 us -> 4.03 us
    all_to_all x1, blocking collectives: 34.3 us -> 37.2 us  [exchange(): lax.all_to_all(tensor, 'seq', split_axis=0, concat_axis=0, tiled=True)]
    unnamed x16 -> x22, local copies, waits for them, and re-layouts: 1.86 us -> 3.99 us
where the time goes in v4:
time: 199 us; the launch traced here: 198 us
  Pallas kernels  70.1 us (35%)
  waiting for transfers between devices  51.2 us (26%)
  blocking collectives  37.2 us (19%)
  starting transfers between devices  35.3 us (18%)
  local copies, waits for them, and re-layouts  4.03 us (2%)
    all_to_all x3, waiting for transfers between devices, exchange(): lax.all_to_all(tensor, 'seq', split_axis=0, concat_axis=0, tiled=True)  47.8 us
    all_to_all x1, blocking collectives, exchange(): lax.all_to_all(tensor, 'seq', split_axis=0, concat_axis=0, tiled=True)  37.2 us
    all_to_all x3, starting transfers between devices, exchange(): lax.all_to_all(tensor, 'seq', split_axis=0, concat_axis=0, tiled=True)  23.6 us
    pallas_call x2, Pallas kernels, window_attention(): pl.pallas_call(window_kernel, grid_spec=pltpu.PrefetchScalarGridSpec(num_...  22.2 us
    pallas_call x1, Pallas kernels, pack_front(): pl.pallas_call(front_kernel, grid_spec=pltpu.PrefetchScalarGridSpec(num_s...  16.5 us
    ppermute x5, starting transfers between devices, butterfly(): return sums + lax.ppermute(sums, 'head', pairs)  11.8 us
    pallas_call x2, Pallas kernels, pack_norms(): pl.pallas_call(functools.partial(pack_norm_kernel, first), grid_spec=pltp...  10.9 us
    pallas_call x1, Pallas kernels, frame_attention(): pl.pallas_call(frame_kernel, grid_spec=pltpu.PrefetchScalarGridSpec(num_s...  8.94 us
  transfers between devices with their start and end apart: 8, of which 6 were waited for; matrix products, arithmetic and copies ran while one was open for 0% of the time, Pallas kernels for 16%

profile of v4, /device:TPU:1, one launch (start us, length us, event | category | flops | bytes accessed | tf_op | source)
XLA Modules:
  0.0 198.2 jit_solution(15842163604774404360)
XLA Ops:
  0.0 2.1 %copy-done = bf16[3072,640]{1,0:T(8,128)(2,1)S(1)} copy-done((bf16[3072,640]{1,0:T(8,128)(2,1)S(1)}, bf16[3072,640]{1,0:T(8,128)(2,1)}, u32[]{:S(2)}) %copy-start) | copy-done | bytes 3932184
  2.1 3.3 %square_sums.1 = f32[2,2,12,128]{3,2,1,0:T(8,128)S(1)} custom-call(bf16[3072,640]{1,0:T(8,128)(2,1)S(1)} %copy-done, bf16[3072,640]{1,0:T(8,128)(2,1)} %k_ref.9), custom_call_target="tpu_custom_call" | custom-call | flops 7864320 | bytes 7864320 | tf_op jit(solution)/shard_map/square_sums/pallas_call | solution.py:66
  5.4 1.5 collective-permute-start
  6.9 0.9 collective-permute-done
  7.8 3.6 %collective-permute-start.1 = (f32[2,2,12,128]{3,2,1,0:T(8,128)S(1)}, f32[2,2,12,128]{3,2,1,0:T(8,128)S(1)}, u32[]{:S(2)}, u32[]{:S(2)}) collective-permute-start(f32[2,2,12,128]{3,2,1,0:T(8,128)S(1)} %add.24), channel_id=1, source_target_pairs={{1,3},{3,1},{5,7},{7,5},{9,11},{11,9},{13,15},{15,13},{17,19},{19,... | collective-permute-start | bytes 73736 | tf_op jit(solution)/shard_map/ppermute | solution.py:541
  11.5 1.2 collective-permute-done.1
  12.7 5.3 %collective-permute-start.2 = (f32[2,2,12,128]{3,2,1,0:T(8,128)S(1)}, f32[2,2,12,128]{3,2,1,0:T(8,128)S(1)}, u32[]{:S(2)}, u32[]{:S(2)}) collective-permute-start(f32[2,2,12,128]{3,2,1,0:T(8,128)S(1)} %add.25), channel_id=1, source_target_pairs={{1,5},{3,7},{5,1},{7,3},{9,13},{11,15},{13,9},{15,11},{17,21},{19,... | collective-permute-start | bytes 73736 | tf_op jit(solution)/shard_map/ppermute | solution.py:541
  18.1 1.2 collective-permute-done.2
  19.4 16.5 %pack_front.1 = (bf16[16,2,2,2,96,128]{5,4,3,2,1,0:T(8,128)(2,1)}, bf16[16,4,2,96,128]{4,3,2,1,0:T(8,128)(2,1)}) custom-call(s32[5]{0:T(128)S(1)} %copy-done.2, s32[1]{0:T(128)} %bitcast.3.odd_ref, s32[12,128]{1,0:T(8,128)S(1)} %bitcast.11, f32[2,2,12,128]{3,2,1,0:T(8,128)S(1)} %add.26.sums_ref, f32[2,1,640]{2,1,0:T(1,128)S(1)} %broadcast_in_dim.31.gain_ref.qg_ref.kg_ref, ...), custom_call_target="tpu_custom_call" | custom-call | flops 7247757312 | bytes 9437184 | tf_op jit(solution)/shard_map/pack_front/pallas_call | solution.py:256
  35.9 6.8 %all-to-all-start = ((bf16[16,4,2,96,128]{4,3,2,1,0:T(8,128)(2,1)}), bf16[16,4,2,96,128]{4,3,2,1,0:T(8,128)(2,1)S(1)}, u32[]{:S(2)}, u32[]{:S(2)}) async-start(bf16[16,4,2,96,128]{4,3,2,1,0:T(8,128)(2,1)} %get-tuple-element.19), calls=%async_computation | async-start | bytes 6291456 | tf_op jit(solution)/shard_map/all_to_all | solution.py:536
  42.7 0.7 collective-permute-start.3
  43.3 0.0 collective-permute-done.3
  43.4 0.7 collective-permute-start.4
  44.0 0.0 collective-permute-done.4
  44.1 0.7 pack_norms.2
  44.7 0.0 copy-start.6
  44.7 24.9 %all-to-all-done.v_ref = bf16[16,4,2,96,128]{4,3,2,1,0:T(8,128)(2,1)S(1)} async-done(((bf16[16,4,2,96,128]{4,3,2,1,0:T(8,128)(2,1)}), bf16[16,4,2,96,128]{4,3,2,1,0:T(8,128)(2,1)S(1)}, u32[]{:S(2)}, u32[]{:S(2)}) %all-to-all-start) | async-done | bytes 3145760 | tf_op jit(solution)/shard_map/all_to_all | solution.py:536
  69.7 1.6 copy-done.5
  71.3 8.5 %all-to-all-start.1 = ((bf16[16,2,2,2,96,128]{5,4,3,2,1,0:T(8,128)(2,1)}), bf16[16,2,2,2,96,128]{5,4,3,2,1,0:T(8,128)(2,1)}, u32[]{:S(2)}, u32[]{:S(2)}) async-start(bf16[16,2,2,2,96,128]{5,4,3,2,1,0:T(8,128)(2,1)} %pack_norms.2), calls=%async_computation.1 | async-start | bytes 6291456 | tf_op jit(solution)/shard_map/all_to_all | solution.py:536
  79.8 0.1 copy.13
  80.0 10.3 %pack_norms.3 = bf16[16,2,2,2,96,128]{5,4,3,2,1,0:T(8,128)(2,1)} custom-call(s32[5]{0:T(128)S(1)} %copy-done.2, s32[1]{0:T(128)} %constant.26.clone.1.turn_ref, s32[12,128]{1,0:T(8,128)S(1)} %bitcast.13, f32[2,2,12,128]{3,2,1,0:T(8,128)S(1)} %add.28.sums_ref, f32[2,1,640]{2,1,0:T(1,128)S(1)} %broadcast_in_dim.31.gain_ref.qg_ref.kg_ref, ...), custom_call_target="tpu_custom_call" | custom-call | flops 4831838208 | bytes 6291456 | tf_op jit(solution)/shard_map/pack_norms/pallas_call | solution.py:288
  90.3 8.9 %frame_attention.1 = bf16[3072,128]{1,0:T(8,128)(2,1)S(1)} custom-call(s32[5]{0:T(128)S(1)} %copy-done.2, f32[5,12,128]{2,1,0:T(8,128)S(1)} %pad.9.bias_ref, f32[2,2,12,128]{3,2,1,0:T(8,128)S(1)} %add.28.sums_ref, f32[2,1,640]{2,1,0:T(1,128)S(1)} %broadcast_in_dim.31.gain_ref.qg_ref.kg_ref, f32[2,1,640]{2,1,0:T(1,128)S(1)} %broadcast_in_dim.31.gain_ref.qg_ref.kg_ref, ...), custom_call_target="tpu_custom_call" | custom-call | flops 4831838208 | bytes 3145728 | tf_op jit(solution)/shard_map/frame_attention/pallas_call | solution.py:440
  99.3 0.0 copy-start.7
  99.3 7.7 %all-to-all-done.1.q_ref.k_ref = bf16[16,2,2,2,96,128]{5,4,3,2,1,0:T(8,128)(2,1)} async-done(((bf16[16,2,2,2,96,128]{5,4,3,2,1,0:T(8,128)(2,1)}), bf16[16,2,2,2,96,128]{5,4,3,2,1,0:T(8,128)(2,1)}, u32[]{:S(2)}, u32[]{:S(2)}) %all-to-all-start.1) | async-done | bytes 3145760 | tf_op jit(solution)/shard_map/all_to_all | solution.py:536
  107.0 0.0 copy-done.3
  107.0 8.3 %all-to-all-start.2 = ((bf16[16,2,2,2,96,128]{5,4,3,2,1,0:T(8,128)(2,1)}), bf16[16,2,2,2,96,128]{5,4,3,2,1,0:T(8,128)(2,1)}, u32[]{:S(2)}, u32[]{:S(2)}) async-start(bf16[16,2,2,2,96,128]{5,4,3,2,1,0:T(8,128)(2,1)} %pack_norms.3), calls=%async_computation.2 | async-start | bytes 6291456 | tf_op jit(solution)/shard_map/all_to_all | solution.py:536
  115.3 0.1 copy.14
  115.4 11.1 %window_attention.2.rest_0_ = bf16[16,4,2,96,128]{4,3,2,1,0:T(8,128)(2,1)S(1)} custom-call(s32[5]{0:T(128)S(1)} %copy-done.2, f32[5,32,128]{2,1,0:T(8,128)S(1)} %bitcast.9, bf16[16,2,2,2,96,128]{5,4,3,2,1,0:T(8,128)(2,1)} %all-to-all-done.1.q_ref.k_ref, bf16[16,2,2,2,96,128]{5,4,3,2,1,0:T(8,128)(2,1)} %all-to-all-done.1.q_ref.k_ref, ...), custom_call_target="tpu_custom_call" | custom-call | flops 6442450944 | bytes 6291456 | tf_op jit(solution)/shard_map/window_attention/pallas_call | solution.py:384
  126.5 15.2 %all-to-all-done.2.q_ref.k_ref = bf16[16,2,2,2,96,128]{5,4,3,2,1,0:T(8,128)(2,1)} async-done(((bf16[16,2,2,2,96,128]{5,4,3,2,1,0:T(8,128)(2,1)}), bf16[16,2,2,2,96,128]{5,4,3,2,1,0:T(8,128)(2,1)}, u32[]{:S(2)}, u32[]{:S(2)}) %all-to-all-start.2) | async-done | bytes 3145760 | tf_op jit(solution)/shard_map/all_to_all | solution.py:536
  141.7 11.1 %window_attention.3 = bf16[16,4,2,96,128]{4,3,2,1,0:T(8,128)(2,1)S(1)} custom-call(s32[5]{0:T(128)S(1)} %copy-done.2, f32[5,32,128]{2,1,0:T(8,128)S(1)} %bitcast.10, bf16[16,2,2,2,96,128]{5,4,3,2,1,0:T(8,128)(2,1)} %all-to-all-done.2.q_ref.k_ref, bf16[16,2,2,2,96,128]{5,4,3,2,1,0:T(8,128)(2,1)} %all-to-all-done.2.q_ref.k_ref, ...), custom_call_target="tpu_custom_call", output_to_operand_aliasing={{}: (5, {})} | custom-call | flops 6442450944 | bytes 6291456 | tf_op jit(solution)/shard_map/window_attention/pallas_call | solution.py:384
  152.8 37.2 %all_to_all.20.moved_ref = bf16[16,4,2,96,128]{4,3,2,1,0:T(8,128)(2,1)S(1)} all-to-all(bf16[16,4,2,96,128]{4,3,2,1,0:T(8,128)(2,1)S(1)} %window_attention.3), channel_id=1, replica_groups=mesh['seq'=16,'head'=8] {'seq'}, dimensions={0} | all-to-all | bytes 6291456 | tf_op jit(solution)/shard_map/all_to_all | solution.py:536
  190.0 8.2 %join.1 = bf16[2,1536,640]{2,1,0:T(8,128)(2,1)} custom-call(s32[5]{0:T(128)S(1)} %copy-done.2, s32[12,128]{1,0:T(8,128)S(1)} %bitcast.14, bf16[16,4,2,96,128]{4,3,2,1,0:T(8,128)(2,1)S(1)} %all_to_all.20.moved_ref, bf16[2,1536,128]{2,1,0:T(8,128)(2,1)S(1)} %bitcast.15), custom_call_target="tpu_custom_call" | custom-call | flops 4831838208 | bytes 7864320 | tf_op jit(solution)/shard_map/join/pallas_call | solution.py:505
  (31 shorter events, 0.2 us)
Async XLA Ops:
  0.0 2.1 %copy-start = (bf16[3072,640]{1,0:T(8,128)(2,1)S(1)}, bf16[3072,640]{1,0:T(8,128)(2,1)}, u32[]{:S(2)}) copy-start(bf16[3072,640]{1,0:T(8,128)(2,1)} %q_ref.9) | copy-start | bytes 11796484
  2.1 9.3 %copy-start.8 = (f32[640]{0:T(1024)S(1)}, f32[640]{0:T(1024)}, u32[]{:S(2)}) copy-start(f32[640]{0:T(1024)} %param.12) | copy-start | bytes 7684
  2.1 9.3 %copy-start.9 = (f32[640]{0:T(1024)S(1)}, f32[640]{0:T(1024)}, u32[]{:S(2)}) copy-start(f32[640]{0:T(1024)} %param.13) | copy-start | bytes 7684
  2.1 17.2 %copy-start.1 = (s32[1536]{0:T(1024)S(1)}, s32[1536]{0:T(1024)}, u32[]{:S(2)}) copy-start(s32[1536]{0:T(1024)} %param.17) | copy-start | bytes 18436
  2.1 17.2 %copy-start.2 = (s32[5]{0:T(128)S(1)}, s32[5]{0:T(128)}, u32[]{:S(2)}) copy-start(s32[5]{0:T(128)} %class_ref.13) | copy-start | bytes 64
  5.4 2.4 %collective-permute-start = (f32[2,2,12,128]{3,2,1,0:T(8,128)S(1)}, f32[2,2,12,128]{3,2,1,0:T(8,128)S(1)}, u32[]{:S(2)}, u32[]{:S(2)}) collective-permute-start(f32[2,2,12,128]{3,2,1,0:T(8,128)S(1)} %square_sums.1), channel_id=1, source_target_pairs={{0,1},{1,0},{2,3},{3,2},{4,5},{5,4},{6,7},{7,6},{8,9},{9,8},{10,11... | collective-permute-start | bytes 73736 | tf_op jit(solution)/shard_map/ppermute | solution.py:541
  7.8 4.9 %collective-permute-start.1 = (f32[2,2,12,128]{3,2,1,0:T(8,128)S(1)}, f32[2,2,12,128]{3,2,1,0:T(8,128)S(1)}, u32[]{:S(2)}, u32[]{:S(2)}) collective-permute-start(f32[2,2,12,128]{3,2,1,0:T(8,128)S(1)} %add.24), channel_id=1, source_target_pairs={{1,3},{3,1},{5,7},{7,5},{9,11},{11,9},{13,15},{15,13},{17,19},{19,... | collective-permute-start | bytes 73736 | tf_op jit(solution)/shard_map/ppermute | solution.py:541
  12.7 6.6 %collective-permute-start.2 = (f32[2,2,12,128]{3,2,1,0:T(8,128)S(1)}, f32[2,2,12,128]{3,2,1,0:T(8,128)S(1)}, u32[]{:S(2)}, u32[]{:S(2)}) collective-permute-start(f32[2,2,12,128]{3,2,1,0:T(8,128)S(1)} %add.25), channel_id=1, source_target_pairs={{1,5},{3,7},{5,1},{7,3},{9,13},{11,15},{13,9},{15,11},{17,21},{19,... | collective-permute-start | bytes 73736 | tf_op jit(solution)/shard_map/ppermute | solution.py:541
  35.9 33.8 %all-to-all-start = ((bf16[16,4,2,96,128]{4,3,2,1,0:T(8,128)(2,1)}), bf16[16,4,2,96,128]{4,3,2,1,0:T(8,128)(2,1)S(1)}, u32[]{:S(2)}, u32[]{:S(2)}) async-start(bf16[16,4,2,96,128]{4,3,2,1,0:T(8,128)(2,1)} %get-tuple-element.19), calls=%async_computation | async-start | bytes 6291456 | tf_op jit(solution)/shard_map/all_to_all | solution.py:536
  42.7 0.7 collective-permute-start.3
  43.4 0.7 collective-permute-start.4
  44.7 35.1 %copy-start.6 = (s32[5,12,12]{2,1,0:T(8,128)S(1)}, s32[5,12,12]{2,1,0:T(8,128)}, u32[]{:S(2)}) copy-start(s32[5,12,12]{2,1,0:T(8,128)} %param.15) | copy-start | bytes 8644
  69.7 1.6 copy-start.5
  71.3 35.7 %all-to-all-start.1 = ((bf16[16,2,2,2,96,128]{5,4,3,2,1,0:T(8,128)(2,1)}), bf16[16,2,2,2,96,128]{5,4,3,2,1,0:T(8,128)(2,1)}, u32[]{:S(2)}, u32[]{:S(2)}) async-start(bf16[16,2,2,2,96,128]{5,4,3,2,1,0:T(8,128)(2,1)} %pack_norms.2), calls=%async_computation.1 | async-start | bytes 6291456 | tf_op jit(solution)/shard_map/all_to_all | solution.py:536
  99.3 7.7 %copy-start.3 = (bf16[3072,128]{1,0:T(8,128)(2,1)}, bf16[3072,128]{1,0:T(8,128)(2,1)S(1)}, u32[]{:S(2)}) copy-start(bf16[3072,128]{1,0:T(8,128)(2,1)S(1)} %frame_attention.1) | copy-start | bytes 2359300
  99.3 16.1 %copy-start.7 = (s32[5,8,8]{2,1,0:T(8,128)S(1)}, s32[5,8,8]{2,1,0:T(8,128)}, u32[]{:S(2)}) copy-start(s32[5,8,8]{2,1,0:T(8,128)} %param.16) | copy-start | bytes 3844
  107.0 34.7 %all-to-all-start.2 = ((bf16[16,2,2,2,96,128]{5,4,3,2,1,0:T(8,128)(2,1)}), bf16[16,2,2,2,96,128]{5,4,3,2,1,0:T(8,128)(2,1)}, u32[]{:S(2)}, u32[]{:S(2)}) async-start(bf16[16,2,2,2,96,128]{5,4,3,2,1,0:T(8,128)(2,1)} %pack_norms.3), calls=%async_computation.2 | async-start | bytes 6291456 | tf_op jit(solution)/shard_map/all_to_all | solution.py:536
  152.8 37.2 %copy-start.4 = (bf16[3072,128]{1,0:T(8,128)(2,1)S(1)}, bf16[3072,128]{1,0:T(8,128)(2,1)}, u32[]{:S(2)}) copy-start(bf16[3072,128]{1,0:T(8,128)(2,1)} %copy-done.3) | copy-start | bytes 2359300
